TPU v7x, 32 devices: a whole 2x2x4 slice. The times are simulated.
32 devices in a mesh: dp: 8 (over z, y), seq: 4 (over x, core).
Axes of the slice: x: 2, y: 2, z: 4, core: 2. Of those that a mesh axis runs over, the one named last changes fastest.
Arguments:
- decoder_in: bfloat16 [16, 2048, 512], P('dp', 'seq'), may hold values from -6 to 6
- source_states: bfloat16 [16, 512, 512], P('dp', 'seq'), may hold values from -6 to 6
- source_len: int32 [16], replicated, may hold values from 128 to 512, as said below
- upsample: int32 [16], replicated, may hold values from 2 to 4, as said below
- send_counts: int32 [8], replicated, may hold values from 0 to 1, as said below
- self_query: bfloat16 [512, 512], P('dp', 'seq'), may hold values from -0.25 to 0.25
- self_key: bfloat16 [512, 512], P('dp', 'seq'), may hold values from -0.25 to 0.25
- self_value: bfloat16 [512, 512], P('dp', 'seq'), may hold values from -0.25 to 0.25
- self_output: bfloat16 [512, 512], P('dp', 'seq'), may hold values from -6 to 6
- cross_query: bfloat16 [512, 512], P('dp', 'seq'), may hold values from -0.25 to 0.25
- cross_key: bfloat16 [512, 512], P('dp', 'seq'), may hold values from -0.25 to 0.25
- cross_value: bfloat16 [512, 512], P('dp', 'seq'), may hold values from -0.25 to 0.25
- cross_output: bfloat16 [512, 512], P('dp', 'seq'), may hold values from -3 to 3
- ffn_expand: bfloat16 [512, 2048], P('dp', 'seq'), may hold values from -0.25 to 0.25
- ffn_reduce: bfloat16 [2048, 512], P('dp', 'seq'), may hold values from -0.125 to 0.125
- norm_gains: bfloat16 [3, 512], P(None, 'seq'), may hold values from 0.5 to 1.5
- out_grad: bfloat16 [16, 2048, 512], P('dp', 'seq'), may hold values from -6 to 6
Outputs:
- decoder_out: bfloat16 [16, 2048, 512], P('dp', 'seq')
- grad_decoder: float32 [16, 2048, 512], P('dp', 'seq')
- grad_source: float32 [16, 512, 512], P('dp', 'seq')
- grad_self_query: float32 [512, 512], P('dp', 'seq')
- grad_self_key: float32 [512, 512], P('dp', 'seq')
- grad_self_value: float32 [512, 512], P('dp', 'seq')
- grad_self_output: float32 [512, 512], P('dp', 'seq')
- grad_cross_query: float32 [512, 512], P('dp', 'seq')
- grad_cross_key: float32 [512, 512], P('dp', 'seq')
- grad_cross_value: float32 [512, 512], P('dp', 'seq')
- grad_cross_output: float32 [512, 512], P('dp', 'seq')
- grad_ffn_expand: float32 [512, 2048], P('dp', 'seq')
- grad_ffn_reduce: float32 [2048, 512], P('dp', 'seq')
- grad_norm_gains: float32 [3, 512], P(None, 'seq')
Inputs may be any that keep to these rules, and one draw needn't show every extreme that they name: `source_len`: in every group of 2 sentences held by one index of dp on entry, one sentence, drawn from the seed and never the last one where that group's send count is 1, has source length 512 and upsample factor 4. `upsample`: each factor is 2 or 4, and 2 occurs in every draw. Where send_counts[g] is 1, index g of dp hands its last sentence to index (g + 4) mod 8. Indices 0, 3, 4 and 7 always hand one, index 5 never does.
All inputs are finite; a program needn't handle non-finite values.
Results may differ from a plain program's by a relative error of at most 0.02.
Values may be sent and summed in bfloat16 or wider, within the bound.
A program may use at most 192 MiB of HBM per device.

v0:
```python
from functools import partial

import jax
import jax.numpy as jnp
from jax import lax
from jax.sharding import PartitionSpec as P

HEADS = 8
DEC = 2048


epsilon = 1e-05
negative = -1000000000.0


def passed_along(value, axis, steps):
    count = lax.axis_size(axis)
    pairs = [(source, (source + steps) % count) for source in range(count)]
    return lax.ppermute(value, axis, pairs)


def normalize(values, gain):
    row_mean = jnp.mean(values, axis=-1, keepdims=True)
    centred = values - row_mean
    spread = jnp.mean(centred * centred, axis=-1, keepdims=True)
    inverse = lax.rsqrt(spread + epsilon)
    scaled = centred * inverse
    return (scaled * gain, scaled, inverse)


def norm_back(upstream, scaled, inverse, gain):
    gain_grad = jnp.sum(upstream * scaled, axis=(0, 1))
    inner_grad = upstream * gain
    centred = inner_grad - jnp.mean(inner_grad, axis=-1, keepdims=True)
    projected = scaled * jnp.mean(inner_grad * scaled, axis=-1, keepdims=True)
    return (inverse * (centred - projected), gain_grad)


def project(values, weight):
    flat_rows = values.reshape(-1, values.shape[-1])
    product = jnp.dot(flat_rows, weight, preferred_element_type=jnp.float32)
    return product.reshape(values.shape[:-1] + (weight.shape[1],))


def project_back(upstream, weight):
    flat_rows = upstream.reshape(-1, upstream.shape[-1])
    product = lax.dot_general(
        flat_rows, weight, (((1,), (1,)), ((), ())), preferred_element_type=jnp.float32
    )
    return product.reshape(upstream.shape[:-1] + (weight.shape[0],))


def weight_grad(values, upstream):
    left_rows = values.reshape(-1, values.shape[-1])
    right_rows = upstream.reshape(-1, upstream.shape[-1])
    return lax.dot_general(
        left_rows, right_rows, (((0,), (0,)), ((), ())), preferred_element_type=jnp.float32
    )


def to_groups(values, seq_size):
    return values.reshape(values.shape[0], values.shape[1], seq_size, values.shape[2] // seq_size)


def to_heads(values, head_count):
    return values.reshape(
        values.shape[0], values.shape[1], head_count, values.shape[3] // head_count
    )


def from_heads(values):
    return values.reshape(values.shape[0], values.shape[1], 1, values.shape[2] * values.shape[3])


def masked_scores(queries, key_rows, key_mask, score_scale):
    scores = (
        jnp.einsum("qhd,khd->hqk", queries, key_rows, preferred_element_type=jnp.float32)
        * score_scale
    )
    return jnp.where(key_mask[None, None, :], scores, negative)


def attend(queries, key_rows, value_rows, key_len):
    length, head_count, head_width = queries.shape
    block_rows = min(512, length)
    block_count = length // block_rows
    score_scale = head_width ** (-0.5)
    key_mask = jnp.arange(key_rows.shape[0]) < key_len
    blocks = queries.reshape(block_count, block_rows, head_count, head_width)
    starts = jnp.arange(block_count) * block_rows

    def compute(query_block):
        scores = masked_scores(query_block, key_rows, key_mask, score_scale)
        row_peak = jnp.max(scores, axis=-1, keepdims=True)
        exp_scores = jnp.exp(scores - row_peak)
        row_total = jnp.sum(exp_scores, axis=-1, keepdims=True)
        weights = (exp_scores / row_total).astype(jnp.bfloat16)
        mixed_heads = jnp.einsum(
            "hqk,khd->qhd", weights, value_rows, preferred_element_type=jnp.float32
        )
        return (mixed_heads.astype(jnp.bfloat16), row_peak[..., 0] + jnp.log(row_total[..., 0]))

    def block_step(entries):
        query_block, block_start = entries
        return compute(query_block)

    mixed_heads, logsum = lax.map(block_step, (blocks, starts))
    return (mixed_heads.reshape(length, head_count, head_width), logsum)


def attend_back(queries, key_rows, value_rows, grad_mixed, logsum, key_len):
    length, head_count, head_width = queries.shape
    block_rows = min(512, length)
    block_count = length // block_rows
    score_scale = head_width ** (-0.5)
    key_mask = jnp.arange(key_rows.shape[0]) < key_len
    blocks = queries.reshape(block_count, block_rows, head_count, head_width)
    grad_blocks = grad_mixed.reshape(block_count, block_rows, head_count, head_width)
    starts = jnp.arange(block_count) * block_rows

    def compute(entries):
        query_block, grad_block, logsum_block = entries
        scores = masked_scores(query_block, key_rows, key_mask, score_scale)
        probs = jnp.exp(scores - logsum_block[..., None])
        value_grad = jnp.einsum(
            "hqk,qhd->khd",
            probs.astype(jnp.bfloat16),
            grad_block,
            preferred_element_type=jnp.float32,
        )
        prob_grad = jnp.einsum(
            "qhd,khd->hqk", grad_block, value_rows, preferred_element_type=jnp.float32
        )
        score_grad = probs * (prob_grad - jnp.sum(prob_grad * probs, axis=-1, keepdims=True))
        score_low = (score_grad * score_scale).astype(jnp.bfloat16)
        query_grad = jnp.einsum(
            "hqk,khd->qhd", score_low, key_rows, preferred_element_type=jnp.float32
        )
        key_grad = jnp.einsum(
            "hqk,qhd->khd", score_low, query_block, preferred_element_type=jnp.float32
        )
        return (query_grad, key_grad, value_grad)

    def block_step(totals, entries):
        key_total, value_total = totals
        members = (entries[0], entries[1], entries[2])
        query_grad, key_grad, value_grad = compute(members)
        return ((key_total + key_grad, value_total + value_grad), query_grad)

    zeros_keys = jnp.zeros(key_rows.shape, jnp.float32)
    (key_total, value_total), query_grads = lax.scan(
        block_step, (zeros_keys, zeros_keys), (blocks, grad_blocks, logsum, starts)
    )
    return (
        query_grads.reshape(length, head_count, head_width).astype(jnp.bfloat16),
        key_total.astype(jnp.bfloat16),
        value_total.astype(jnp.bfloat16),
    )


def row_sums(
    part_zero,
    part_one,
    part_two,
    part_three,
    part_four,
    part_five,
    part_six,
    part_seven,
    part_eight,
    part_nine,
    part_gains,
):
    return (
        lax.psum_scatter(part_zero, "dp", scatter_dimension=0, tiled=True),
        lax.psum_scatter(part_one, "dp", scatter_dimension=0, tiled=True),
        lax.psum_scatter(part_two, "dp", scatter_dimension=0, tiled=True),
        lax.psum_scatter(part_three, "dp", scatter_dimension=0, tiled=True),
        lax.psum_scatter(part_four, "dp", scatter_dimension=0, tiled=True),
        lax.psum_scatter(part_five, "dp", scatter_dimension=0, tiled=True),
        lax.psum_scatter(part_six, "dp", scatter_dimension=0, tiled=True),
        lax.psum_scatter(part_seven, "dp", scatter_dimension=0, tiled=True),
        lax.psum_scatter(part_eight, "dp", scatter_dimension=0, tiled=True),
        lax.psum_scatter(part_nine, "dp", scatter_dimension=0, tiled=True),
        lax.psum_scatter(part_gains, "dp", scatter_dimension=0, tiled=True),
    )


def column_sums(
    part_zero,
    part_one,
    part_two,
    part_three,
    part_four,
    part_five,
    part_six,
    part_seven,
    part_eight,
    part_nine,
    part_ten,
):
    return (
        lax.psum_scatter(
            part_zero.astype(jnp.bfloat16), "seq", scatter_dimension=1, tiled=True
        ).astype(jnp.float32),
        lax.psum_scatter(
            part_one.astype(jnp.bfloat16), "seq", scatter_dimension=1, tiled=True
        ).astype(jnp.float32),
        lax.psum_scatter(
            part_two.astype(jnp.bfloat16), "seq", scatter_dimension=1, tiled=True
        ).astype(jnp.float32),
        lax.psum_scatter(
            part_three.astype(jnp.bfloat16), "seq", scatter_dimension=1, tiled=True
        ).astype(jnp.float32),
        lax.psum_scatter(
            part_four.astype(jnp.bfloat16), "seq", scatter_dimension=1, tiled=True
        ).astype(jnp.float32),
        lax.psum_scatter(
            part_five.astype(jnp.bfloat16), "seq", scatter_dimension=1, tiled=True
        ).astype(jnp.float32),
        lax.psum_scatter(
            part_six.astype(jnp.bfloat16), "seq", scatter_dimension=1, tiled=True
        ).astype(jnp.float32),
        lax.psum_scatter(
            part_seven.astype(jnp.bfloat16), "seq", scatter_dimension=1, tiled=True
        ).astype(jnp.float32),
        lax.psum_scatter(
            part_eight.astype(jnp.bfloat16), "seq", scatter_dimension=1, tiled=True
        ).astype(jnp.float32),
        lax.psum_scatter(
            part_nine.astype(jnp.bfloat16), "seq", scatter_dimension=1, tiled=True
        ).astype(jnp.float32),
        lax.psum_scatter(
            part_ten.astype(jnp.bfloat16), "seq", scatter_dimension=1, tiled=True
        ).astype(jnp.float32),
    )


def replace_last(home_rows, returned_rows, use_returned, home_count):
    last_rows = jnp.where(use_returned, returned_rows, home_rows[home_count - 1])
    return jnp.concatenate([home_rows[: home_count - 1], last_rows[None]], 0)


def body(
    decoder_in,
    source_states,
    source_len,
    upsample,
    send_counts,
    self_query,
    self_key,
    self_value,
    self_output,
    cross_query,
    cross_key,
    cross_value,
    cross_output,
    ffn_expand,
    ffn_reduce,
    norm_gains,
    out_grad,
):
    seq_size = lax.axis_size("seq")
    dp_size = lax.axis_size("dp")
    half_way = dp_size // 2
    group_index = lax.axis_index("dp")
    partner_index = (group_index + half_way) % dp_size
    home_count, rows_dec, model_width = decoder_in.shape
    rows_src = source_states.shape[1]
    head_count = HEADS // seq_size
    sending = send_counts[group_index]
    taking = send_counts[partner_index]
    outgoing = jnp.concatenate(
        [decoder_in[home_count - 1], source_states[home_count - 1], out_grad[home_count - 1]], 0
    )
    arrived = passed_along(outgoing, "dp", half_way)
    decoder_slots = jnp.concatenate([decoder_in, arrived[:rows_dec][None]], 0)
    source_slots = jnp.concatenate(
        [source_states, arrived[rows_dec : rows_dec + rows_src][None]], 0
    )
    cotangent_slots = jnp.concatenate([out_grad, arrived[rows_dec + rows_src :][None]], 0)
    own_len = lax.dynamic_slice_in_dim(source_len, group_index * home_count, home_count)
    own_up = lax.dynamic_slice_in_dim(upsample, group_index * home_count, home_count)
    keeping = (jnp.arange(home_count) < home_count - 1) | (sending == 0)
    kept_len = jnp.where(keeping, own_len, 0)
    far_slot = partner_index * home_count + home_count - 1
    far_len = jnp.where(taking == 1, source_len[far_slot], 0)
    slot_len = jnp.concatenate([kept_len, far_len[None]], 0)
    slot_up = jnp.concatenate([own_up, upsample[far_slot][None]], 0)
    dec_len = slot_len * slot_up
    group_tokens = jnp.sum(dec_len)
    loss_scale = jnp.float32(DEC) / group_tokens.astype(jnp.float32)
    sentence_count = home_count + 1
    positions = lax.axis_index("seq") * rows_dec + jnp.arange(rows_dec)
    row_mask = (positions[None, :] < dec_len[:, None]).astype(jnp.float32)[..., None]
    columns = (
        lax.all_gather(self_query, "seq", axis=1, tiled=True),
        lax.all_gather(self_key, "seq", axis=1, tiled=True),
        lax.all_gather(self_value, "seq", axis=1, tiled=True),
        lax.all_gather(self_output, "seq", axis=1, tiled=True),
        lax.all_gather(cross_query, "seq", axis=1, tiled=True),
        lax.all_gather(cross_key, "seq", axis=1, tiled=True),
        lax.all_gather(cross_value, "seq", axis=1, tiled=True),
        lax.all_gather(cross_output, "seq", axis=1, tiled=True),
        lax.all_gather(ffn_expand, "seq", axis=1, tiled=True),
        lax.all_gather(ffn_reduce, "seq", axis=1, tiled=True),
        lax.all_gather(norm_gains, "seq", axis=1, tiled=True),
    )
    whole_weights = (
        lax.all_gather(columns[0], "dp", axis=0, tiled=True),
        lax.all_gather(columns[1], "dp", axis=0, tiled=True),
        lax.all_gather(columns[2], "dp", axis=0, tiled=True),
        lax.all_gather(columns[3], "dp", axis=0, tiled=True),
        lax.all_gather(columns[4], "dp", axis=0, tiled=True),
        lax.all_gather(columns[5], "dp", axis=0, tiled=True),
        lax.all_gather(columns[6], "dp", axis=0, tiled=True),
        lax.all_gather(columns[7], "dp", axis=0, tiled=True),
        lax.all_gather(columns[8], "dp", axis=0, tiled=True),
        lax.all_gather(columns[9], "dp", axis=0, tiled=True),
    )
    (
        query_self,
        key_self,
        value_self,
        output_self,
        query_cross,
        key_cross,
        value_cross,
        output_cross,
        expand_whole,
        reduce_whole,
    ) = whole_weights
    gain_rows = columns[10].astype(jnp.float32)
    inputs = decoder_slots.astype(jnp.float32)
    normed, scaled_one, inverse_one = normalize(inputs, gain_rows[0])
    hidden_one = normed.astype(jnp.bfloat16)
    head_parts = (
        lax.all_to_all(
            to_groups(project(hidden_one, query_self).astype(jnp.bfloat16), seq_size),
            "seq",
            split_axis=2,
            concat_axis=1,
            tiled=True,
        ),
        lax.all_to_all(
            to_groups(project(hidden_one, key_self).astype(jnp.bfloat16), seq_size),
            "seq",
            split_axis=2,
            concat_axis=1,
            tiled=True,
        ),
        lax.all_to_all(
            to_groups(project(hidden_one, value_self).astype(jnp.bfloat16), seq_size),
            "seq",
            split_axis=2,
            concat_axis=1,
            tiled=True,
        ),
        lax.all_to_all(
            to_groups(project(source_slots, key_cross).astype(jnp.bfloat16), seq_size),
            "seq",
            split_axis=2,
            concat_axis=1,
            tiled=True,
        ),
        lax.all_to_all(
            to_groups(project(source_slots, value_cross).astype(jnp.bfloat16), seq_size),
            "seq",
            split_axis=2,
            concat_axis=1,
            tiled=True,
        ),
    )
    self_q, self_k, self_v, cross_k, cross_v = [
        to_heads(member, head_count) for member in head_parts
    ]
    self_mixed, self_logsum = lax.map(
        lambda entries: attend(entries[0], entries[1], entries[2], entries[3]),
        (self_q, self_k, self_v, dec_len),
    )
    self_rows = lax.all_to_all(
        from_heads(self_mixed), "seq", split_axis=1, concat_axis=2, tiled=True
    ).reshape(sentence_count, rows_dec, model_width)
    after_self = inputs + project(self_rows, output_self)
    normed, scaled_two, inverse_two = normalize(after_self, gain_rows[1])
    hidden_two = normed.astype(jnp.bfloat16)
    cross_query_rows = to_groups(project(hidden_two, query_cross).astype(jnp.bfloat16), seq_size)
    cross_q = to_heads(
        lax.all_to_all(cross_query_rows, "seq", split_axis=2, concat_axis=1, tiled=True), head_count
    )
    cross_mixed, cross_logsum = lax.map(
        lambda entries: attend(entries[0], entries[1], entries[2], entries[3]),
        (cross_q, cross_k, cross_v, slot_len, dec_len),
    )
    cross_rows = lax.all_to_all(
        from_heads(cross_mixed), "seq", split_axis=1, concat_axis=2, tiled=True
    ).reshape(sentence_count, rows_dec, model_width)
    after_cross = after_self + project(cross_rows, output_cross)
    normed, scaled_three, inverse_three = normalize(after_cross, gain_rows[2])
    hidden_three = normed.astype(jnp.bfloat16)
    expanded = project(hidden_three, expand_whole)
    activated = jax.nn.gelu(expanded, approximate=True).astype(jnp.bfloat16)
    final = after_cross + project(activated, reduce_whole)
    decoder_out = (final * row_mask).astype(jnp.bfloat16)
    grad_final = cotangent_slots.astype(jnp.float32) * row_mask * loss_scale
    grad_ffn = grad_final.astype(jnp.bfloat16)
    local_ffn_reduce = weight_grad(activated, grad_ffn)
    grad_activated = project_back(grad_ffn, reduce_whole)
    _, pullback = jax.vjp(partial(jax.nn.gelu, approximate=True), expanded)
    grad_expanded = pullback(grad_activated)[0].astype(jnp.bfloat16)
    local_ffn_expand = weight_grad(hidden_three, grad_expanded)
    back_three, gain_three = norm_back(
        project_back(grad_expanded, expand_whole), scaled_three, inverse_three, gain_rows[2]
    )
    grad_after_cross = grad_final + back_three
    cross_branch = grad_after_cross.astype(jnp.bfloat16)
    local_cross_output = weight_grad(cross_rows, cross_branch)
    grad_cross_mixed = project_back(cross_branch, output_cross).astype(jnp.bfloat16)
    cross_grad_heads = to_heads(
        lax.all_to_all(
            to_groups(grad_cross_mixed, seq_size), "seq", split_axis=2, concat_axis=1, tiled=True
        ),
        head_count,
    )
    cross_dq, cross_dk, cross_dv = lax.map(
        lambda entries: attend_back(
            entries[0], entries[1], entries[2], entries[3], entries[4], entries[5]
        ),
        (cross_q, cross_k, cross_v, cross_grad_heads, cross_logsum, slot_len, dec_len),
    )
    cross_dq_rows = lax.all_to_all(
        from_heads(cross_dq), "seq", split_axis=1, concat_axis=2, tiled=True
    ).reshape(sentence_count, rows_dec, model_width)
    local_cross_query = weight_grad(hidden_two, cross_dq_rows)
    back_two, gain_two = norm_back(
        project_back(cross_dq_rows, query_cross), scaled_two, inverse_two, gain_rows[1]
    )
    grad_after_self = grad_after_cross + back_two
    self_branch = grad_after_self.astype(jnp.bfloat16)
    local_self_output = weight_grad(self_rows, self_branch)
    grad_self_mixed = project_back(self_branch, output_self).astype(jnp.bfloat16)
    self_grad_heads = to_heads(
        lax.all_to_all(
            to_groups(grad_self_mixed, seq_size), "seq", split_axis=2, concat_axis=1, tiled=True
        ),
        head_count,
    )
    self_dq, self_dk, self_dv = lax.map(
        lambda entries: attend_back(
            entries[0], entries[1], entries[2], entries[3], entries[4], entries[5]
        ),
        (self_q, self_k, self_v, self_grad_heads, self_logsum, dec_len),
    )
    returned = (
        lax.all_to_all(from_heads(self_dq), "seq", split_axis=1, concat_axis=2, tiled=True),
        lax.all_to_all(from_heads(self_dk), "seq", split_axis=1, concat_axis=2, tiled=True),
        lax.all_to_all(from_heads(self_dv), "seq", split_axis=1, concat_axis=2, tiled=True),
        lax.all_to_all(from_heads(cross_dk), "seq", split_axis=1, concat_axis=2, tiled=True),
        lax.all_to_all(from_heads(cross_dv), "seq", split_axis=1, concat_axis=2, tiled=True),
    )
    rows_dq, rows_dk, rows_dv, source_dk, source_dv = [
        member.reshape(sentence_count, -1, model_width) for member in returned
    ]
    local_self_query = weight_grad(hidden_one, rows_dq)
    local_self_key = weight_grad(hidden_one, rows_dk)
    local_self_value = weight_grad(hidden_one, rows_dv)
    grad_hidden_one = (
        project_back(rows_dq, query_self)
        + project_back(rows_dk, key_self)
        + project_back(rows_dv, value_self)
    )
    back_one, gain_one = norm_back(grad_hidden_one, scaled_one, inverse_one, gain_rows[0])
    grad_decoder = grad_after_self + back_one
    local_cross_key = weight_grad(source_slots, source_dk)
    local_cross_value = weight_grad(source_slots, source_dv)
    grad_source = project_back(source_dk, key_cross) + project_back(source_dv, value_cross)
    homeward = jnp.concatenate(
        [
            decoder_out[home_count].astype(jnp.float32),
            grad_decoder[home_count],
            grad_source[home_count],
        ],
        0,
    )
    came_back = passed_along(homeward.astype(jnp.bfloat16), "dp", half_way).astype(homeward.dtype)
    use_returned = sending == 1
    decoder_home = replace_last(
        decoder_out[:home_count],
        came_back[:rows_dec].astype(jnp.bfloat16),
        use_returned,
        home_count,
    )
    grad_decoder_home = replace_last(
        grad_decoder[:home_count], came_back[rows_dec : 2 * rows_dec], use_returned, home_count
    )
    grad_source_home = replace_last(
        grad_source[:home_count], came_back[2 * rows_dec :], use_returned, home_count
    )
    gain_local = jnp.stack([gain_one, gain_two, gain_three])
    partial_rows = row_sums(
        local_self_query,
        local_self_key,
        local_self_value,
        local_self_output,
        local_cross_query,
        local_cross_key,
        local_cross_value,
        local_cross_output,
        local_ffn_expand,
        local_ffn_reduce,
        jnp.tile(gain_local, (dp_size, 1)),
    )
    reduced = column_sums(
        partial_rows[0],
        partial_rows[1],
        partial_rows[2],
        partial_rows[3],
        partial_rows[4],
        partial_rows[5],
        partial_rows[6],
        partial_rows[7],
        partial_rows[8],
        partial_rows[9],
        partial_rows[10],
    )
    return (
        decoder_home,
        grad_decoder_home,
        grad_source_home,
        reduced[0],
        reduced[1],
        reduced[2],
        reduced[3],
        reduced[4],
        reduced[5],
        reduced[6],
        reduced[7],
        reduced[8],
        reduced[9],
        reduced[10],
    )


def solution(mesh):
    placed = (
        P("dp", "seq", None),
        P("dp", "seq", None),
        P(),
        P(),
        P(),
        P("dp", "seq"),
        P("dp", "seq"),
        P("dp", "seq"),
        P("dp", "seq"),
        P("dp", "seq"),
        P("dp", "seq"),
        P("dp", "seq"),
        P("dp", "seq"),
        P("dp", "seq"),
        P("dp", "seq"),
        P(None, "seq"),
        P("dp", "seq", None),
    )
    return jax.shard_map(
        body,
        mesh=mesh,
        in_specs=placed,
        out_specs=(
            P("dp", "seq", None),
            P("dp", "seq", None),
            P("dp", "seq", None),
            P("dp", "seq"),
            P("dp", "seq"),
            P("dp", "seq"),
            P("dp", "seq"),
            P("dp", "seq"),
            P("dp", "seq"),
            P("dp", "seq"),
            P("dp", "seq"),
            P("dp", "seq"),
            P("dp", "seq"),
            P(None, "seq"),
        ),
        check_vma=False,
    )
```

profile of v0, /device:TPU:0, one launch (start us, length us, event | category | flops | bytes accessed | tf_op | source)
XLA Modules:
  0.0 2302.9 jit_solution(4327691607315356908)
XLA Ops:
  24.5 63.7 %all_gather.69 = bf16[512,512]{1,0:T(8,128)(2,1)S(1)} all-gather(bf16[64,512]{1,0:T(8,128)(2,1)S(1)} %all_gather.68), channel_id=1, replica_groups=mesh['dp'=8,'seq'=4] {'dp'}, dimensions={0}, use_global_device_ids=true | all-gather | bytes 589824 | tf_op jit(solution)/shard_map/all_gather | solution.py:312
  119.9 31.5 %all_gather.67 = bf16[512,512]{1,0:T(8,128)(2,1)S(1)} all-gather(bf16[64,512]{1,0:T(8,128)(2,1)S(1)} %all_gather.66), channel_id=1, replica_groups=mesh['dp'=8,'seq'=4] {'dp'}, dimensions={0}, use_global_device_ids=true | all-gather | bytes 589824 | tf_op jit(solution)/shard_map/all_gather | solution.py:311
  178.7 31.4 %all_gather.65 = bf16[512,512]{1,0:T(8,128)(2,1)S(1)} all-gather(bf16[64,512]{1,0:T(8,128)(2,1)S(1)} %all_gather.64), channel_id=1, replica_groups=mesh['dp'=8,'seq'=4] {'dp'}, dimensions={0}, use_global_device_ids=true | all-gather | bytes 589824 | tf_op jit(solution)/shard_map/all_gather | solution.py:310
  269.5 34.3 %all_gather.77 = bf16[512,512]{1,0:T(8,128)(2,1)} all-gather(bf16[64,512]{1,0:T(8,128)(2,1)S(1)} %all_gather.76), channel_id=1, replica_groups=mesh['dp'=8,'seq'=4] {'dp'}, dimensions={0}, use_global_device_ids=true | all-gather | bytes 589824 | tf_op jit(solution)/shard_map/all_gather | solution.py:316
  321.8 109.1 %while.109 = (s32[]{:T(128)}, bf16[3,2048,2,64]{1,3,2,0:T(8,128)(2,1)}, f32[3,4,2,512]{3,2,1,0:T(2,128)S(1)}, bf16[3,2048,2,64]{1,3,2,0:T(8,128)(2,1)}, bf16[3,2...) while((s32[]{:T(128)}, ...), condition=%wide.region_7.8_spmd, body=%wide.region_2.0_spmd.sunk | while | flops 562103296 | bytes 37036376 | solution.py:377
  362.3 28.3 %while.116 = (s32[]{:T(128)}, bf16[4,512,2,64]{1,3,2,0:T(8,128)(2,1)}, f32[4,2,512]{2,1,0:T(2,128)S(1)}, bf16[4,512,2,64]{1,3,2,0:T(8,128)(2,1)S(1)}, bf16[2048,...) while((s32[]{:T(128)}, bf16[4,512,2,64]{1,3,2,0:T(8,128)(2,1)}, ...), condition=%wide.region_6.6_spmd.clone, body=%wide.region_3.5_spmd.clone.sunk | while | flops 562103296 | bytes 28614792 | solution.py:107
  440.0 31.8 %all_gather.75 = bf16[512,512]{1,0:T(8,128)(2,1)S(1)} all-gather(bf16[64,512]{1,0:T(8,128)(2,1)S(1)} %copy-done.84), channel_id=1, replica_groups=mesh['dp'=8,'seq'=4] {'dp'}, dimensions={0}, use_global_device_ids=true | all-gather | bytes 589824 | tf_op jit(solution)/shard_map/all_gather | solution.py:315
  471.8 33.6 %all_gather.73 = bf16[512,512]{1,0:T(8,128)(2,1)} all-gather(bf16[64,512]{1,0:T(8,128)(2,1)S(1)} %copy-done.83), channel_id=1, replica_groups=mesh['dp'=8,'seq'=4] {'dp'}, dimensions={0}, use_global_device_ids=true | all-gather | bytes 589824 | tf_op jit(solution)/shard_map/all_gather | solution.py:314
  505.5 33.5 %all_gather.71 = bf16[512,512]{1,0:T(8,128)(2,1)} all-gather(bf16[64,512]{1,0:T(8,128)(2,1)S(1)} %copy-done.82), channel_id=1, replica_groups=mesh['dp'=8,'seq'=4] {'dp'}, dimensions={0}, use_global_device_ids=true | all-gather | bytes 589824 | tf_op jit(solution)/shard_map/all_gather | solution.py:313
  602.2 48.9 %while.111 = (s32[]{:T(128)}, bf16[3,2048,2,64]{1,3,2,0:T(8,128)(2,1)}, f32[3,4,2,512]{3,2,1,0:T(2,128)}, bf16[3,2048,2,64]{1,3,2,0:T(8,128)(2,1)S(1)}, bf16[3,5...) while((s32[]{:T(128)}, ...), condition=%wide.region_15.16_spmd, body=%wide.region_10.15_spmd.sunk | while | flops 140574208 | bytes 14223706 | solution.py:391
  687.4 33.8 %all_gather.79 = bf16[512,512]{1,0:T(8,128)(2,1)} all-gather(bf16[64,512]{1,0:T(8,128)(2,1)S(1)} %all_gather.78), channel_id=1, replica_groups=mesh['dp'=8,'seq'=4] {'dp'}, dimensions={0}, use_global_device_ids=true | all-gather | bytes 589824 | tf_op jit(solution)/shard_map/all_gather | solution.py:317
  792.4 165.7 %while.113 = (s32[]{:T(128)}, bf16[3,2048,2,64]{1,3,2,0:T(8,128)(2,1)}, bf16[3,512,2,64]{1,3,2,0:T(8,128)(2,1)}, bf16[3,512,2,64]{1,3,2,0:T(8,128)(2,1)}, bf16[3...) while((s32[]{:T(128)}, ...), condition=%wide.region_25.26_spmd, body=%wide.region_21.25_spmd.sunk | while | flops 343281152 | bytes 40285716 | solution.py:425
  799.8 44.8 %while.118 = (s32[]{:T(128)}, f32[512,2,64]{0,2,1:T(8,128)}, f32[512,2,64]{0,2,1:T(8,128)S(1)}, bf16[4,512,2,64]{1,3,2,0:T(8,128)(2,1)S(1)}, bf16[4,512,2,64]{1,...) while((s32[]{:T(128)}, f32[512,2,64]{0,2,1:T(8,128)}, ...), condition=%wide.region_24.24_spmd.clone, body=%wide.region_22.23_spmd.clone.sunk | while | flops 343150080 | bytes 25310372 | solution.py:151
  855.1 44.7 %while.118 = (s32[]{:T(128)}, f32[512,2,64]{0,2,1:T(8,128)}, f32[512,2,64]{0,2,1:T(8,128)S(1)}, bf16[4,512,2,64]{1,3,2,0:T(8,128)(2,1)S(1)}, bf16[4,512,2,64]{1,...) while((s32[]{:T(128)}, f32[512,2,64]{0,2,1:T(8,128)}, ...), condition=%wide.region_24.24_spmd.clone, body=%wide.region_22.23_spmd.clone.sunk | while | flops 343150080 | bytes 25310372 | solution.py:151
  910.3 44.7 %while.118 = (s32[]{:T(128)}, f32[512,2,64]{0,2,1:T(8,128)}, f32[512,2,64]{0,2,1:T(8,128)S(1)}, bf16[4,512,2,64]{1,3,2,0:T(8,128)(2,1)S(1)}, bf16[4,512,2,64]{1,...) while((s32[]{:T(128)}, f32[512,2,64]{0,2,1:T(8,128)}, ...), condition=%wide.region_24.24_spmd.clone, body=%wide.region_22.23_spmd.clone.sunk | while | flops 343150080 | bytes 25310372 | solution.py:151
  1076.4 534.1 %while.115 = (s32[]{:T(128)}, bf16[3,2048,2,64]{1,3,2,0:T(8,128)(2,1)}, bf16[3,2048,2,64]{1,3,2,0:T(8,128)(2,1)}, bf16[3,2048,2,64]{1,3,2,0:T(8,128)(2,1)}, bf16...) while((s32[]{:T(128)}, ...), condition=%wide.region_32.33_spmd, body=%wide.region_28.32_spmd.sunk | while | flops 1398284288 | bytes 147136992 | solution.py:448
  1083.1 165.4 %while.119 = (s32[]{:T(128)}, f32[2048,2,64]{0,2,1:T(8,128)}, f32[2048,2,64]{0,2,1:T(8,128)S(1)}, bf16[4,512,2,64]{1,3,2,0:T(8,128)(2,1)}, bf16[4,512,2,64]{1,3,...) while((s32[]{:T(128)}, f32[2048,2,64]{0,2,1:T(8,128)}, ...), condition=%wide.region_31.31_spmd.clone, body=%wide.region_29.30_spmd.clone.sunk | while | flops 1397760000 | bytes 132423880 | solution.py:151
  1261.4 165.0 %while.119 = (s32[]{:T(128)}, f32[2048,2,64]{0,2,1:T(8,128)}, f32[2048,2,64]{0,2,1:T(8,128)S(1)}, bf16[4,512,2,64]{1,3,2,0:T(8,128)(2,1)}, bf16[4,512,2,64]{1,3,...) while((s32[]{:T(128)}, f32[2048,2,64]{0,2,1:T(8,128)}, ...), condition=%wide.region_31.31_spmd.clone, body=%wide.region_29.30_spmd.clone.sunk | while | flops 1397760000 | bytes 132423880 | solution.py:151
  1439.3 165.0 %while.119 = (s32[]{:T(128)}, f32[2048,2,64]{0,2,1:T(8,128)}, f32[2048,2,64]{0,2,1:T(8,128)S(1)}, bf16[4,512,2,64]{1,3,2,0:T(8,128)(2,1)}, bf16[4,512,2,64]{1,3,...) while((s32[]{:T(128)}, f32[2048,2,64]{0,2,1:T(8,128)}, ...), condition=%wide.region_31.31_spmd.clone, body=%wide.region_29.30_spmd.clone.sunk | while | flops 1397760000 | bytes 132423880 | solution.py:151
  1613.6 28.3 %all_to_all.240 = bf16[3,2048,1,128]{3,0,2,1:T(4,128)(2,1)S(1)} all-to-all(bf16[3,2048,1,128]{3,0,2,1:T(4,128)(2,1)S(1)} %copy.268), channel_id=1, replica_groups=mesh['dp'=8,'seq'=4] {'seq'}, dimensions={1} | all-to-all | bytes 3145728 | tf_op jit(solution)/shard_map/all_to_all | solution.py:457
  1742.0 33.9 %all-reduce = bf16[24,512]{1,0:T(8,128)(2,1)S(1)} all-reduce(f32[24,512]{1,0:T(8,128)S(1)} %tile.10), channel_id=22, replica_groups=mesh['dp'=8,'seq'=4] {'dp'}, use_global_device_ids=true, to_apply=%region_58.59.clone | all-reduce | flops 12288 | bytes 73728
  1822.0 47.2 %reduce-scatter.44.cloned.1.call-done = f32[64,512]{1,0:T(8,128)} async-done(((f32[512,512]{1,0:T(8,128)}), f32[64,512]{1,0:T(8,128)}) %reduce-scatter.44.cloned.1.call-update) | async-done | bytes 131088 | tf_op jit(solution)/shard_map/reduce_scatter | solution.py:176
  2002.5 88.4 %reduce-scatter.62.cloned.1.call-done = f32[256,512]{1,0:T(8,128)} async-done(((f32[2048,512]{1,0:T(8,128)}), f32[256,512]{1,0:T(8,128)}) %reduce-scatter.62.cloned.1.call-update) | async-done | bytes 524304 | tf_op jit(solution)/shard_map/reduce_scatter | solution.py:184
  2098.1 84.4 %reduce-scatter.58.cloned.1.call-done = f32[64,2048]{1,0:T(8,128)} async-done(((f32[512,2048]{1,0:T(8,128)}), f32[64,2048]{1,0:T(8,128)}) %reduce-scatter.58.cloned.1.call-update) | async-done | bytes 524304 | tf_op jit(solution)/shard_map/reduce_scatter | solution.py:183
  (1103 shorter events, 1790.8 us)
Async XLA Ops:
  218.7 513.0 %all-gather.3.cloned.1.call-start = ((), (), s32[]{:S(2)}) async-start(), calls=%async_computation.37 | async-start | bytes 2359296 | tf_op jit(solution)/shard_map/all_gather | solution.py:318
  570.6 169.5 %all-gather.5.cloned.1.call-start = ((), (), s32[]{:S(2)}) async-start(), calls=%async_computation.38 | async-start | bytes 2359296 | tf_op jit(solution)/shard_map/all_gather | solution.py:319
  767.1 951.2 %reduce-scatter.56.cloned.1.call-start = ((), (), s32[]{:S(2)}) async-start(), calls=%async_computation.46 | async-start | bytes 1179648 | tf_op jit(solution)/shard_map/reduce_scatter | solution.py:182
  963.6 756.6 %reduce-scatter.52.cloned.1.call-start = ((), (), s32[]{:S(2)}) async-start(), calls=%async_computation.44 | async-start | bytes 1179648 | tf_op jit(solution)/shard_map/reduce_scatter | solution.py:180
  991.4 730.6 %reduce-scatter.54.cloned.1.call-start = ((), (), s32[]{:S(2)}) async-start(), calls=%async_computation.45 | async-start | bytes 1179648 | tf_op jit(solution)/shard_map/reduce_scatter | solution.py:181
  994.1 729.8 %reduce-scatter.50.cloned.1.call-start = ((), (), s32[]{:S(2)}) async-start(), calls=%async_computation.43 | async-start | bytes 1179648 | tf_op jit(solution)/shard_map/reduce_scatter | solution.py:179
  1046.7 680.2 %reduce-scatter.48.cloned.1.call-start = ((), (), s32[]{:S(2)}) async-start(), calls=%async_computation.42 | async-start | bytes 1179648 | tf_op jit(solution)/shard_map/reduce_scatter | solution.py:178
  1048.8 769.6 %reduce-scatter.46.cloned.1.call-start = ((), (), s32[]{:S(2)}) async-start(), calls=%async_computation.41 | async-start | bytes 1179648 | tf_op jit(solution)/shard_map/reduce_scatter | solution.py:177
  1646.5 173.7 %reduce-scatter.42.cloned.1.call-start = ((), (), s32[]{:S(2)}) async-start(), calls=%async_computation.39 | async-start | bytes 1179648 | tf_op jit(solution)/shard_map/reduce_scatter | solution.py:175
  1682.4 186.8 %reduce-scatter.44.cloned.1.call-start = ((), (), s32[]{:S(2)}) async-start(), calls=%async_computation.40 | async-start | bytes 1179648 | tf_op jit(solution)/shard_map/reduce_scatter | solution.py:176
  1718.3 171.1 %reduce-scatter.78.cloned.1.call-start = ((), (), s32[]{:S(2)}) async-start(), calls=%async_computation.57 | async-start | bytes 163840
  1720.1 191.2 %reduce-scatter.74.cloned.1.call-start = ((), (), s32[]{:S(2)}) async-start(), calls=%async_computation.55 | async-start | bytes 163840
  1721.9 211.5 %reduce-scatter.76.cloned.1.call-start = ((), (), s32[]{:S(2)}) async-start(), calls=%async_computation.56 | async-start | bytes 163840
  1723.8 231.6 %reduce-scatter.72.cloned.1.call-start = ((), (), s32[]{:S(2)}) async-start(), calls=%async_computation.54 | async-start | bytes 163840
  1725.6 251.7 %reduce-scatter.70.cloned.1.call-start = ((), (), s32[]{:S(2)}) async-start(), calls=%async_computation.53 | async-start | bytes 163840
  1728.6 270.7 %reduce-scatter.82.cloned.1.call-start = ((), (), s32[]{:S(2)}) async-start(), calls=%async_computation.59 | async-start | bytes 163840
  1776.7 314.2 %reduce-scatter.62.cloned.1.call-start = ((), (), s32[]{:S(2)}) async-start(), calls=%async_computation.49 | async-start | bytes 4718592 | tf_op jit(solution)/shard_map/reduce_scatter | solution.py:184
  1786.4 396.1 %reduce-scatter.58.cloned.1.call-start = ((), (), s32[]{:S(2)}) async-start(), calls=%async_computation.47 | async-start | bytes 4718592 | tf_op jit(solution)/shard_map/reduce_scatter | solution.py:183
  1796.7 407.6 %reduce-scatter.68.cloned.1.call-start = ((), (), s32[]{:S(2)}) async-start(), calls=%async_computation.52 | async-start | bytes 163840
  1818.3 182.4 %collective-permute-start.1 = (bf16[1152,512]{1,0:T(8,128)(2,1)S(1)}, bf16[1152,512]{1,0:T(8,128)(2,1)S(1)}, u32[]{:S(2)}, u32[]{:S(2)}) collective-permute-start(bf16[1152,512]{1,0:T(8,128)(2,1)S(1)} %pad_maximum_fusion.4), channel_id=1, source_target_pairs={{0,16},{4,20},{8,24},{12,28},{16,0},{20,4},{24,8},{28,12},{1,17},{... | collective-permute-start | bytes 3538952 | tf_op jit(solution)/shard_map/ppermute | solution.py:19
  1820.1 406.8 %reduce-scatter.64.cloned.1.call-start = ((), (), s32[]{:S(2)}) async-start(), calls=%async_computation.50 | async-start | bytes 163840
  1821.9 427.6 %reduce-scatter.66.cloned.1.call-start = ((), (), s32[]{:S(2)}) async-start(), calls=%async_computation.51 | async-start | bytes 163840
  1870.9 401.3 %reduce-scatter.80.cloned.1.call-start = ((), (), s32[]{:S(2)}) async-start(), calls=%async_computation.58 | async-start | bytes 327680
  2092.9 201.8 %reduce-scatter.60.cloned.1.call-start = ((), (), s32[]{:S(2)}) async-start(), calls=%async_computation.48 | async-start | bytes 327680 | tf_op jit(solution)/shard_map/reduce_scatter | solution.py:227
  (186 other events, 2449.1 us)
Sparse Core Ops, SparseCore 0:
  241.6 52.3 all-gather.2
  593.5 45.8 all-gather.4
  771.3 61.2 reduce-scatter.55
  974.5 59.6 reduce-scatter.51
  1037.5 62.4 reduce-scatter.53
  1103.7 62.4 reduce-scatter.49
  1169.6 62.3 reduce-scatter.47
  1646.6 59.7 reduce-scatter.45
  1710.4 62.6 reduce-scatter.41
  1776.8 92.3 reduce-scatter.43
  1871.6 17.7 reduce-scatter.77
  1891.7 19.5 reduce-scatter.73
  1913.8 19.5 reduce-scatter.75
  1935.8 19.5 reduce-scatter.71
  1957.7 19.5 reduce-scatter.69
  1979.7 19.5 reduce-scatter.81
  2002.8 88.0 reduce-scatter.61
  2094.8 87.6 reduce-scatter.57
  2184.9 19.2 reduce-scatter.67
  2207.3 19.5 reduce-scatter.63
  2229.9 19.5 reduce-scatter.65
  2252.1 20.0 reduce-scatter.79
  2274.6 19.9 reduce-scatter.59
where the time goes:
time: 2320 us; the launch traced here: 2300 us
  matrix products  768 us (33%)
  blocking collectives  559 us (24%)
  waiting for transfers between devices  517 us (22%)
  local copies, waits for them, and re-layouts  262 us (11%)
  other arithmetic  119 us (5%)
  starting transfers between devices  55.7 us (2%)
    dot_general x24, matrix products, compute(): jnp.einsum('hqk,khd->qhd', score_low, key_rows, preferred_element_type=jn...  232 us
    dot_general x24, matrix products, compute(): jnp.einsum('hqk,qhd->khd', score_low, query_block, preferred_element_type...  225 us
    unnamed x33, waiting for transfers between devices  199 us
    reduce_scatter x1, waiting for transfers between devices, row_sums(): lax.psum_scatter(part_nine, 'dp', scatter_dimension=0, tiled=True)  88.4 us
    reduce_scatter x1, waiting for transfers between devices, row_sums(): lax.psum_scatter(part_eight, 'dp', scatter_dimension=0, tiled=True)  84.4 us
    dot_general x24, matrix products, compute(): jnp.einsum('qhd,khd->hqk', grad_block, value_rows, preferred_element_type...  76.3 us
    all_gather x1, blocking collectives, body(): lax.all_gather(columns[2], 'dp', axis=0, tiled=True)  63.7 us
    dot_general x48, matrix products, masked_scores(): jnp.einsum('qhd,khd->hqk', queries, key_rows, preferred_element_type=jnp....  58.4 us
  transfers between devices with their start and end apart: 38, of which 20 were waited for; matrix products, arithmetic and copies ran while one was open for 47% of the time, Pallas kernels for 0%

commit v1 on v0

v1 whole, which is shorter than its diff:
```python
from functools import partial

import jax
import jax.numpy as jnp
from jax import lax
from jax.experimental import pallas as pl
from jax.experimental.pallas import tpu as pltpu
from jax.sharding import PartitionSpec as P

HEADS = 8
EPSILON = 1e-05
NEGATIVE = -1000000000.0
LOG2E = 1.4426950408889634
LN2 = 0.6931471805599453
GELU_IN = 0.7978845608028654
GELU_CUBE = 0.044715
BLOCK = 256
PAIR = 128

bf16 = jnp.bfloat16
f32 = jnp.float32
VMEM = pltpu.VMEM
VMEM_LIMIT = 60 * 1024 * 1024
PARAMS = pltpu.CompilerParams(vmem_limit_bytes=VMEM_LIMIT)


def dot(left, right):
    return jnp.dot(left, right, preferred_element_type=f32)


def dot_nt(left, right):
    return lax.dot_general(left, right, (((1,), (1,)), ((), ())), preferred_element_type=f32)


def block_at(index, size):
    return pl.ds(pl.multiple_of(index * size, size), size)


def row_mean(values):
    return jnp.mean(values, axis=-1, keepdims=True)


def normalize(values):
    centred = values - row_mean(values)
    inverse = lax.rsqrt(row_mean(centred * centred) + EPSILON)
    return centred * inverse, inverse


def norm_back(upstream, scaled, inverse, gain):
    inner = upstream * gain
    back = inverse * (inner - row_mean(inner) - scaled * row_mean(inner * scaled))
    return back, jnp.sum(upstream * scaled, axis=0, keepdims=True)


def three_parts(column, lane, last):
    high = column.astype(bf16).astype(f32)
    middle = (column - high).astype(bf16).astype(f32)
    low = column - high - middle
    rest = jnp.where(lane == 3, last, 0.0)
    return jnp.where(
        lane == 0, high, jnp.where(lane == 1, middle, jnp.where(lane == 2, low, rest))
    ).astype(bf16)


def one_head(values, first, head):
    zero = jnp.zeros_like(values)
    return jnp.where(first, values, zero) if head == 0 else jnp.where(first, zero, values)


def attend_pair(query, keys, key_extra, values, lane):
    first = lane < 64
    ones = jnp.where(lane == 3, 1.0, 0.0).astype(bf16)
    keys = jnp.concatenate([keys, key_extra], axis=1)
    scores = [
        dot_nt(jnp.concatenate([one_head(query, first, head), ones], axis=1), keys)
        for head in (0, 1)
    ]
    mixed, extras = [], []
    for head in (0, 1):
        peak = jnp.max(scores[head], axis=1, keepdims=True)
        exps = jnp.exp2(scores[head] - peak)
        total = jnp.sum(exps, axis=1, keepdims=True)
        mixed.append(dot(exps.astype(bf16), values) * (1.0 / total))
        extras.append(three_parts(-(peak + jnp.log2(total)), lane, 1.0))
    return jnp.where(first, mixed[0], mixed[1]).astype(bf16), extras


def attend_pair_back(
    query, grad, mixed, query_extra, key_at, value_at, key_columns_at, chunks, lane, add_key, add_value
):
    first = lane < 64
    product = grad.astype(f32) * mixed.astype(f32)
    queries = [one_head(query, first, head) for head in (0, 1)]
    grads = [one_head(grad, first, head) for head in (0, 1)]
    long_queries = [jnp.concatenate([queries[h], query_extra[h]], axis=1) for h in (0, 1)]
    long_grads = []
    for head in (0, 1):
        delta = jnp.sum(one_head(product, first, head), axis=1, keepdims=True)
        long_grads.append(
            jnp.concatenate([grads[head], three_parts(-delta, lane, 0.0)], axis=1)
        )
    both_queries = jnp.concatenate(queries, axis=0)
    both_grads = jnp.concatenate(grads, axis=0)
    query_grads = [jnp.zeros((64, query.shape[0]), f32)] * 2
    for chunk in range(chunks):
        keys, values = key_at(chunk), value_at(chunk)
        probs, score_grads = [], []
        for head in (0, 1):
            prob = jnp.exp2(dot_nt(keys, long_queries[head]))
            score_grad = (prob * dot_nt(values, long_grads[head])).astype(bf16)
            probs.append(prob.astype(bf16))
            score_grads.append(score_grad)
            query_grads[head] = query_grads[head] + dot(key_columns_at(chunk, head), score_grad)
        add_value(chunk, dot(jnp.concatenate(probs, axis=1), both_grads))
        add_key(chunk, dot(jnp.concatenate(score_grads, axis=1), both_queries))
    return (jnp.concatenate(query_grads, axis=0) * 0.125).astype(bf16)


def copy_to(source, target, send, receive, partner):
    return pltpu.make_async_remote_copy(
        src_ref=source,
        dst_ref=target,
        send_sem=send,
        recv_sem=receive,
        device_id=partner,
        device_id_type=pl.DeviceIdType.MESH,
    )


def entry_barrier(partners):
    barrier = pltpu.get_barrier_semaphore()
    for partner in partners:
        pl.semaphore_signal(
            barrier, inc=1, device_id=partner, device_id_type=pl.DeviceIdType.MESH
        )
    pl.semaphore_wait(barrier, len(partners))


class Where:
    def __init__(self, planes):
        group, self.place = lax.axis_index("dp"), lax.axis_index("seq")
        self.group = group
        self.chip, self.core = self.place // 2, self.place % 2
        self.plane, self.side = group // 2, group % 2
        self.planes = planes
        self.other_core = self.at(self.chip, 1 - self.core)
        self.other_chip = self.at(1 - self.chip, self.core)
        self.diagonal = self.at(1 - self.chip, 1 - self.core)
        self.other_side = {"dp": self.plane * 2 + 1 - self.side}
        self.other_planes = [
            {"dp": (self.plane + step) % planes * 2 + self.side} for step in range(1, planes)
        ]

    def at(self, chip, core):
        return {"seq": chip * 2 + core}

    def column(self, step):
        return (self.chip + step // 2) % 2 * 2 + (self.core + step % 2) % 2

    def everyone(self):
        return [self.other_core, self.other_chip, self.diagonal, self.other_side] + self.other_planes


class Semaphores:
    def __init__(self, send, receive):
        self.send, self.receive, self.count = send, receive, 0
        self.sent = []

    def remote(self, source, target, partner):
        at = self.count
        self.count += 1
        copy = copy_to(source, target, self.send.at[at], self.receive.at[at], partner)
        self.sent.append(copy)
        return copy

    def local(self, source, target):
        at = self.count
        self.count += 1
        return pltpu.make_async_copy(source, target, self.send.at[at])


def block_places(where_chip, where_core, rows, offset, index, size):
    per = rows // size
    slot = index // per
    block = (where_chip + slot % 2) % 2 * 2 + (where_core + slot // 2) % 2
    return block * rows + index % per * size + offset


def mask_columns(where_chip, where_core, rows, count, size, length, ref):
    lane = lax.broadcasted_iota(jnp.int32, (size, PAIR), 1)
    offset = lax.broadcasted_iota(jnp.int32, (size, PAIR), 0)

    def step(index, _):
        places = block_places(where_chip, where_core, rows, offset, index, size)
        bias = jnp.where(places < length, 0.0, NEGATIVE)
        ref[block_at(index, size), :] = jnp.where(
            lane < 3, 1.0, jnp.where(lane == 3, bias, 0.0)
        ).astype(bf16)
        return 0

    lax.fori_loop(0, count // size, step, 0)


def open_kernel(
    comm,
    planes,
    deep,
    source_len_ref,
    upsample_ref,
    *refs,
):
    if comm:
        (
            decoder_ref, source_ref, cotangent_ref,
            wq_in, wk_in, wv_in, *later_in, gain_in,
            x_out, source_out, cotangent_out, qkv_out, later_a, later_b, later_c, gain_out,
            q_out, k_out, v_out, mixed_out, extra_out,
            x_ref, qkv_ref, gain_ref, hidden_ref, weight_ref, mask_ref,
            q_ref, k_ref, v_ref, mixed_ref, extra_ref, send, receive,
        ) = refs
    else:
        (
            x_ref, qkv_ref, gain_ref,
            q_out, k_out, v_out, mixed_out, extra_out,
            hidden_ref, weight_ref, mask_ref,
            q_ref, k_ref, v_ref, mixed_ref, extra_ref, send, receive,
        ) = refs
    where = Where(planes)
    place, plane, side, chip, core = where.place, where.plane, where.side, where.chip, where.core
    total, width = x_ref.shape
    pairs = width // PAIR
    own = total // 2
    rows = total // 4
    semaphores = Semaphores(send, receive)
    column = where.column

    if comm:
        group = where.group
        x_slots = [x_ref.at[slot * rows : (slot + 1) * rows] for slot in range(4)]
        few = source_ref.shape[1]
        s_slots = [source_out.at[slot * few : (slot + 1) * few] for slot in range(4)]
        c_slots = [cotangent_out.at[slot * rows : (slot + 1) * rows] for slot in range(2)]
        local_x = semaphores.local(decoder_ref.at[chip], x_slots[0])
        local_gain = semaphores.local(gain_in, gain_ref.at[place])
        mine = qkv_ref.at[place, side, plane]
        local_qkv = [
            semaphores.local(ref, mine.at[at * deep : (at + 1) * deep])
            for at, ref in enumerate((wq_in, wk_in, wv_in))
        ]
        first = [local_x, local_gain, *local_qkv]
        wo_in, wcq_in, wck_in, wcv_in, wco_in, w1_in, w2_in = later_in
        mine_a = later_a.at[place, side, plane]
        mine_b = later_b.at[place, side, plane]
        mine_c = later_c.at[place, side, plane]
        wide = w1_in.shape[1] // PAIR
        local_later = [
            [
                semaphores.local(ref, mine_a.at[at * deep : (at + 1) * deep])
                for at, ref in enumerate((wo_in, wcq_in, wck_in, wcv_in, wco_in))
            ],
            [
                semaphores.local(
                    w1_in.at[:, at * PAIR : (at + 1) * PAIR], mine_b.at[at * deep : (at + 1) * deep]
                )
                for at in range(wide)
            ],
            [semaphores.local(w2_in, mine_c)],
        ]
        local_rest = [
            semaphores.local(source_ref.at[chip], s_slots[0]),
            semaphores.local(cotangent_ref.at[chip], c_slots[0]),
        ]
        for copy in first + local_later[0] + local_later[1] + local_later[2] + local_rest:
            copy.start()
        entry_barrier(where.everyone())

        x_cross = semaphores.remote(decoder_ref.at[1 - chip], x_slots[1], where.other_chip)
        x_core = semaphores.remote(decoder_ref.at[chip], x_slots[2], where.other_core)
        x_pass = semaphores.remote(x_slots[1], x_slots[3], where.other_core)
        s_cross = semaphores.remote(source_ref.at[1 - chip], s_slots[1], where.other_chip)
        s_core = semaphores.remote(source_ref.at[chip], s_slots[2], where.other_core)
        s_pass = semaphores.remote(s_slots[1], s_slots[3], where.other_core)
        c_cross = semaphores.remote(cotangent_ref.at[1 - chip], c_slots[1], where.other_chip)
        gain_sends = [
            semaphores.remote(gain_in, gain_ref.at[place], partner)
            for partner in (where.other_core, where.other_chip, where.diagonal)
        ]
        qkv_planes = [semaphores.remote(mine, mine, partner) for partner in where.other_planes]
        qkv_side = semaphores.remote(
            qkv_ref.at[place, side], qkv_ref.at[place, side], where.other_side
        )
        qkv_core = semaphores.remote(qkv_ref.at[place], qkv_ref.at[place], where.other_core)
        qkv_chip = semaphores.remote(qkv_ref.at[place], qkv_ref.at[place], where.other_chip)
        across = column(2)
        qkv_pass = semaphores.remote(qkv_ref.at[across], qkv_ref.at[across], where.other_core)
        later = []
        for buffer in (later_a, later_b, later_c):
            block = buffer.at[place, side, plane]
            later.append(
                dict(
                    planes=[semaphores.remote(block, block, p) for p in where.other_planes],
                    chip=[
                        semaphores.remote(
                            buffer.at[place, side], buffer.at[place, side], where.other_chip
                        )
                    ],
                    side=[
                        semaphores.remote(
                            buffer.at[at, side], buffer.at[at, side], where.other_side
                        )
                        for at in (place, across)
                    ],
                    core=[
                        semaphores.remote(buffer.at[at], buffer.at[at], where.other_core)
                        for at in (place, across)
                    ],
                )
            )

        def begin(copies):
            for copy in copies:
                copy.start()

        def arrive(copies):
            for copy in copies:
                copy.wait_recv()

        x_cross.start()
        x_core.start()
        for copy in [local_gain, *local_qkv]:
            copy.wait()
        begin(gain_sends)
        begin(qkv_planes)
        begin([s_cross, s_core])
        for copies, piece in zip(local_later, later):
            for copy in copies:
                copy.wait()
            begin(piece["planes"])

    length = source_len_ref[where.group * 2 + chip] * upsample_ref[where.group * 2 + chip]
    mask_columns(chip, core, rows, total, BLOCK, length, mask_ref)

    def hide(slot):
        gain = jnp.concatenate([gain_ref[at, 0:1, :] for at in range(pairs)], axis=1)

        def step(index, _):
            at = block_at(index + slot * (rows // BLOCK), BLOCK)
            scaled, _ = normalize(x_ref[at, :].astype(f32))
            hidden_ref[at, :] = (scaled * gain).astype(bf16)
            return 0

        lax.fori_loop(0, rows // BLOCK, step, 0)

    def take_weights(pair):
        for part in range(3):
            for at in range(8):
                weight_ref[at * 64 : at * 64 + 64, part * PAIR : (part + 1) * PAIR] = qkv_ref[
                    pair, at % 2, at // 2, part * 64 : part * 64 + 64, :
                ]

    def project(pair, slot, count):
        def step(index, _):
            at = block_at(index + slot * (rows // BLOCK), BLOCK)
            both = dot(hidden_ref[at, :], weight_ref[:, PAIR:]).astype(bf16)
            k_ref[pair, at, :] = both[:, :PAIR]
            v_ref[pair, at, :] = both[:, PAIR:]
            return 0

        def query_step(index, _):
            at = block_at(index + slot * (rows // BLOCK), BLOCK)
            query = dot(hidden_ref[at, :], weight_ref[:, :PAIR]) * (0.125 * LOG2E)
            q_ref[pair, at, :] = query.astype(bf16)
            return 0

        lax.fori_loop(0, count * (rows // BLOCK), step, 0)
        if slot < 2:
            lax.fori_loop(0, min(2 - slot, count) * (rows // BLOCK), query_step, 0)

    if comm:
        local_x.wait()
        arrive(gain_sends)
        hide(0)
        arrive([x_core])
        hide(2)
        arrive(qkv_planes)
        qkv_side.start()
        arrive([x_cross])
        x_pass.start()
        hide(1)
        arrive([qkv_side])
        begin([qkv_core, qkv_chip])
        take_weights(place)
        project(place, 0, 1)
        project(place, 2, 1)
        project(place, 1, 1)
        arrive([x_pass])
        hide(3)
        project(place, 3, 1)
    else:
        for slot in range(4):
            hide(slot)
        take_weights(place)
        project(place, 0, 4)

    size = 2 * BLOCK
    blocks = own // size
    lane = lax.broadcasted_iota(jnp.int32, (size, PAIR), 1)

    def outs_of(pair):
        return [
            (q_ref.at[pair], q_out.at[pair]),
            (k_ref.at[pair], k_out.at[pair]),
            (v_ref.at[pair], v_out.at[pair]),
            (mixed_ref.at[pair], mixed_out.at[pair]),
            (extra_ref.at[pair], extra_out.at[pair]),
        ]

    first_out = semaphores.count

    def out_copies(step, pair):
        return [
            pltpu.make_async_copy(source, target, send.at[first_out + step * 5 + at])
            for at, (source, target) in enumerate(outs_of(pair))
        ]

    def when(index, value, todo):
        pl.when(index == value)(todo)

    def step(index, _):
        turn = index // blocks
        pair = column(turn)
        if comm:
            a, b, c = later

            @pl.when(index == 0)
            def _():
                arrive(a["planes"])
                begin(a["chip"])

            @pl.when(index == 1)
            def _():
                arrive(b["planes"])
                begin(b["chip"])
                arrive(c["planes"])
                begin(c["chip"])

            @pl.when(index == 2)
            def _():
                arrive([qkv_core])
                arrive(a["chip"])
                begin(a["side"])

            @pl.when(index == 3)
            def _():
                arrive([qkv_chip])
                qkv_pass.start()
                arrive(b["chip"])
                begin(b["side"])
                local_rest[0].wait()
                arrive([s_cross])
                s_pass.start()
                c_cross.start()

            @pl.when(index == 4)
            def _():
                arrive(c["chip"])
                begin(c["side"])
                arrive(a["side"])
                begin(a["core"])

            @pl.when(index == 6)
            def _():
                arrive([qkv_pass])
                arrive(b["side"])
                begin(b["core"])

        @pl.when((index % blocks == 0) & (index > 0))
        def _():
            take_weights(pair)
            project(pair, 0, 4)

        at = block_at(index % blocks, size)
        mixed, extras = attend_pair(
            q_ref[pair, at, :], k_ref[pair], mask_ref[...], v_ref[pair], lane
        )
        mixed_ref[pair, at, :] = mixed
        extra_ref[pair, 0, at, :] = extras[0]
        extra_ref[pair, 1, at, :] = extras[1]

        @pl.when(index % blocks == blocks - 1)
        def _():
            for copy in out_copies(turn, pair):
                copy.start()

        return 0

    lax.fori_loop(0, pairs * blocks, step, 0)
    if comm:
        x_local = pltpu.make_async_copy(x_ref, x_out, send.at[first_out + 20])
        qkv_local = pltpu.make_async_copy(qkv_ref, qkv_out, send.at[first_out + 21])
        gain_local = pltpu.make_async_copy(gain_ref, gain_out, send.at[first_out + 22])
        for copy in (x_local, qkv_local, gain_local):
            copy.start()
        c = later[2]
        arrive(c["side"])
        begin(c["core"])
        local_rest[1].wait()
        arrive([s_core, s_pass, c_cross])
        for piece in later:
            arrive(piece["core"])
        for copy in semaphores.sent:
            copy.wait_send()
        for copy in (x_local, qkv_local, gain_local):
            copy.wait()
    for turn in range(pairs):
        for copy in out_copies(turn, column(turn)):
            copy.wait()


def whole_weight(ref, blocks, start, count, chunks=1):
    columns, sides, planes = blocks.shape[:3]
    for column in range(columns):
        for side in range(sides):
            for plane in range(planes):
                row = (plane * sides + side) * count
                for chunk in range(chunks):
                    at = (column * chunks + chunk) * PAIR
                    ref[row : row + count, at : at + PAIR] = blocks[
                        column, side, plane, start + chunk * count : start + (chunk + 1) * count, :
                    ]


def middle_kernel(
    planes,
    source_len_ref,
    upsample_ref,
    send_ref,
    x_any,
    mixed_ref,
    cotangent_ref,
    source_ref,
    later_a,
    later_b,
    later_c,
    gain_blocks,
    out_ref,
    grad_mixed_ref,
    grad_self_ref,
    dwo_ref,
    dwcq_ref,
    dwco_ref,
    dw1_ref,
    dw2t_ref,
    dwck_ref,
    dwcv_ref,
    grad_source_ref,
    dgain_ref,
    x_ref,
    wo_ref,
    wcq_ref,
    wck_ref,
    wcv_ref,
    wco_ref,
    w1_ref,
    w2_ref,
    ck_ref,
    cv_ref,
    ckt_ref,
    cextra_ref,
    dck_ref,
    dcv_ref,
    x_sem,
    cm_s,
    extra_s,
    dqt_s,
    dq_s,
    gcm_s,
    qc_s,
):
    rows_own, width = x_ref.shape
    pairs = mixed_ref.shape[0]
    hidden_width = w1_ref.shape[1]
    chunk = 512
    x_copy = pltpu.make_async_copy(x_any.at[:rows_own], x_ref, x_sem)
    x_copy.start()
    where = Where(planes)
    chip, core = where.chip, where.core
    few = source_ref.shape[0]
    deep = width // 8
    for at, ref in enumerate((wo_ref, wcq_ref, wck_ref, wcv_ref, wco_ref)):
        whole_weight(ref, later_a, at * deep, deep)
    whole_weight(w1_ref, later_b, 0, deep, hidden_width // width)
    whole_weight(w2_ref, later_c, 0, hidden_width // 8)
    gain_rows = jnp.concatenate([gain_blocks[at] for at in range(pairs)], axis=1)
    gain_two = gain_rows[1:2, :]
    gain_three = gain_rows[2:3, :]
    lane = lax.broadcasted_iota(jnp.int32, (BLOCK, PAIR), 1)
    offset = lax.broadcasted_iota(jnp.int32, (BLOCK, 1), 0)
    for ref in (dwo_ref, dwcq_ref, dwco_ref, dw1_ref, dw2t_ref, dck_ref, dcv_ref, dgain_ref):
        ref[...] = jnp.zeros(ref.shape, f32)

    dp_size = planes * 2
    group, half_way = where.group, planes
    sentence = group * 2 + chip
    src_len = source_len_ref[sentence]
    dec_len = src_len * upsample_ref[sentence]
    moved = chip * send_ref[group]
    holder = (group + moved * half_way) % dp_size
    partner = (holder + half_way) % dp_size

    def tokens_of(slot):
        return source_len_ref[slot] * upsample_ref[slot]

    tokens = (
        tokens_of(holder * 2)
        + tokens_of(holder * 2 + 1) * (1 - send_ref[holder])
        + tokens_of(partner * 2 + 1) * send_ref[partner]
    )
    loss_scale = jnp.full((1, 1), rows_own * 2, f32) / jnp.full((1, 1), tokens, jnp.int32).astype(f32)
    mask_columns(chip, core, few // 4, few, few // 4, src_len, cextra_ref)

    def source_step(index, _):
        rows = block_at(index, BLOCK)
        source = source_ref[rows, :]
        key_rows = dot(source, wck_ref[...]).astype(bf16)
        value_rows = dot(source, wcv_ref[...]).astype(bf16)
        for pair in range(pairs):
            part = key_rows[:, pair * PAIR : (pair + 1) * PAIR]
            ck_ref[pair, rows, :] = part
            ckt_ref[pair, :, rows] = part.T
            cv_ref[pair, rows, :] = value_rows[:, pair * PAIR : (pair + 1) * PAIR]
        return 0

    lax.fori_loop(0, few // BLOCK, source_step, 0)
    x_copy.wait()

    def step(index, _):
        rows = block_at(index, BLOCK)
        place = block_places(chip, core, rows_own // 2, offset, index, BLOCK)
        counted = jnp.where(place < dec_len, 1.0, 0.0)
        self_rows = jnp.concatenate([mixed_ref[pair, rows, :] for pair in range(pairs)], axis=1)
        after_self = x_ref[rows, :].astype(f32) + dot(self_rows, wo_ref[...])
        scaled_two, inverse_two = normalize(after_self)
        hidden_two = (scaled_two * gain_two).astype(bf16)
        queries = (dot(hidden_two, wcq_ref[...]) * (0.125 * LOG2E)).astype(bf16)
        for pair in range(pairs):
            qc_s[pair] = queries[:, pair * PAIR : (pair + 1) * PAIR]

        def cross(pair, _):
            mixed, extras = attend_pair(
                qc_s[pair], ck_ref[pair], cextra_ref[...], cv_ref[pair], lane
            )
            cm_s[pair] = mixed
            extra_s[2 * pair] = extras[0]
            extra_s[2 * pair + 1] = extras[1]
            return 0

        lax.fori_loop(0, pairs, cross, 0)
        cross_rows = jnp.concatenate([cm_s[pair] for pair in range(pairs)], axis=1)
        after_cross = after_self + dot(cross_rows, wco_ref[...])
        scaled_three, inverse_three = normalize(after_cross)
        hidden_three = (scaled_three * gain_three).astype(bf16)
        grad_final = cotangent_ref[rows, :].astype(f32) * (counted * loss_scale)
        grad_ffn = grad_final.astype(bf16)
        hidden_columns = hidden_three.T
        grad_columns = grad_ffn.T
        final = after_cross
        grad_hidden = jnp.zeros((BLOCK, width), f32)
        for part in range(hidden_width // chunk):
            columns = slice(part * chunk, (part + 1) * chunk)
            expanded = dot(hidden_three, w1_ref[:, columns])
            square = expanded * expanded
            bend = jnp.tanh(GELU_IN * expanded * (1.0 + GELU_CUBE * square))
            half = 0.5 * (1.0 + bend)
            activated = (expanded * half).astype(bf16)
            slope = half + 0.5 * expanded * (1.0 - bend * bend) * (
                GELU_IN * (1.0 + 3.0 * GELU_CUBE * square)
            )
            grad_expanded = (dot_nt(grad_ffn, w2_ref[columns, :]) * slope).astype(bf16)
            final = final + dot(activated, w2_ref[columns, :])
            dw2t_ref[:, columns] += dot(grad_columns, activated)
            dw1_ref[:, columns] += dot(hidden_columns, grad_expanded)
            grad_hidden = grad_hidden + dot_nt(grad_expanded, w1_ref[:, columns])
        out_ref[rows, :] = (final * counted).astype(bf16)
        back, gain_sum = norm_back(grad_hidden, scaled_three, inverse_three, gain_three)
        dgain_ref[2:3, :] += gain_sum
        grad_cross = grad_final + back
        branch = grad_cross.astype(bf16)
        dwco_ref[...] += dot(cross_rows.T, branch)
        grad_mixed = dot_nt(branch, wco_ref[...]).astype(bf16)
        for pair in range(pairs):
            gcm_s[pair] = grad_mixed[:, pair * PAIR : (pair + 1) * PAIR]

        def cross_back(pair, _):
            def add_key(_, value):
                dck_ref[pair] += value

            def add_value(_, value):
                dcv_ref[pair] += value

            extra = cextra_ref[...]
            dqt_s[pair] = attend_pair_back(
                qc_s[pair],
                gcm_s[pair],
                cm_s[pair],
                [extra_s[2 * pair], extra_s[2 * pair + 1]],
                lambda _: jnp.concatenate([ck_ref[pair], extra], axis=1),
                lambda _: jnp.concatenate([cv_ref[pair], extra], axis=1),
                lambda _, head: ckt_ref[pair, 64 * head : 64 * head + 64, :],
                1,
                lane,
                add_key,
                add_value,
            )
            dq_s[pair] = dqt_s[pair].T
            return 0

        lax.fori_loop(0, pairs, cross_back, 0)
        query_grad = jnp.concatenate([dq_s[pair] for pair in range(pairs)], axis=1)
        dwcq_ref[...] += dot(hidden_two.T, query_grad)
        back, gain_sum = norm_back(
            dot_nt(query_grad, wcq_ref[...]), scaled_two, inverse_two, gain_two
        )
        dgain_ref[1:2, :] += gain_sum
        grad_self = grad_cross + back
        grad_self_ref[rows, :] = grad_self
        branch = grad_self.astype(bf16)
        dwo_ref[...] += dot(self_rows.T, branch)
        grad_mixed = dot_nt(branch, wo_ref[...]).astype(bf16)
        for pair in range(pairs):
            grad_mixed_ref[pair, rows, :] = grad_mixed[:, pair * PAIR : (pair + 1) * PAIR]
        return 0

    lax.fori_loop(0, rows_own // BLOCK, step, 0)
    dwck_ref[...] = jnp.zeros(dwck_ref.shape, f32)
    dwcv_ref[...] = jnp.zeros(dwcv_ref.shape, f32)

    def gathered(ref, rows, factor):
        parts = [(ref[pair, rows, :] * factor).astype(bf16) for pair in range(pairs)]
        return jnp.concatenate(parts, axis=1)

    def source_back(index, _):
        rows = block_at(index, BLOCK)
        source_columns = source_ref[rows, :].T
        key_grad = gathered(dck_ref, rows, LN2)
        value_grad = gathered(dcv_ref, rows, 1.0)
        dwck_ref[...] += dot(source_columns, key_grad)
        dwcv_ref[...] += dot(source_columns, value_grad)
        grad_source_ref[rows, :] = dot_nt(key_grad, wck_ref[...]) + dot_nt(
            value_grad, wcv_ref[...]
        )
        return 0

    lax.fori_loop(0, few // BLOCK, source_back, 0)


def self_back_kernel(
    planes,
    source_len_ref,
    upsample_ref,
    q_ref,
    k_ref,
    v_ref,
    mixed_ref,
    grad_ref,
    query_extra_ref,
    dqt_ref,
    dk_ref,
    dv_ref,
    keys_s,
    values_s,
    kt_s,
):
    pairs, rows_own, _ = q_ref.shape
    keys = k_ref.shape[1]
    where = Where(planes)
    sentence = where.group * 2 + where.chip
    length = source_len_ref[sentence] * upsample_ref[sentence]
    extra = values_s.at[:, PAIR:]
    mask_columns(where.chip, where.core, keys // 4, keys, BLOCK, length, extra)
    keys_s[:, PAIR:] = values_s[:, PAIR:]
    size = 2 * BLOCK
    blocks = rows_own // size
    lane = lax.broadcasted_iota(jnp.int32, (size, PAIR), 1)
    chunk = 512

    def step(index, _):
        pair = index // blocks
        rows = block_at(index % blocks, size)

        @pl.when(index % blocks == 0)
        def _():
            dk_ref[pair] = jnp.zeros((keys, PAIR), f32)
            dv_ref[pair] = jnp.zeros((keys, PAIR), f32)
            keys_s[:, :PAIR] = k_ref[pair]
            values_s[:, :PAIR] = v_ref[pair]
            kt_s[...] = k_ref[pair].T

        def part(ref):
            return lambda at: ref[at * chunk : (at + 1) * chunk, :]

        def add_to(ref):
            def add(at, value):
                ref[pair, at * chunk : (at + 1) * chunk, :] += value

            return add

        dqt_ref[pair, :, rows] = attend_pair_back(
            q_ref[pair, rows, :],
            grad_ref[pair, rows, :],
            mixed_ref[pair, rows, :],
            [query_extra_ref[pair, head, rows, :] for head in (0, 1)],
            part(keys_s),
            part(values_s),
            lambda at, head: kt_s[64 * head : 64 * head + 64, at * chunk : (at + 1) * chunk],
            keys // chunk,
            lane,
            add_to(dk_ref),
            add_to(dv_ref),
        )
        return 0

    lax.fori_loop(0, pairs * blocks, step, 0)


def close_kernel(
    own,
    x_ref,
    qkv_ref,
    gain_blocks,
    dqt_ref,
    dk_ref,
    dv_ref,
    grad_self_ref,
    own_ref,
    other_ref,
    dwq_ref,
    dwk_ref,
    dwv_ref,
    dgain_ref,
    wq_ref,
    wk_ref,
    wv_ref,
):
    pairs = dk_ref.shape[0]
    gain = jnp.concatenate([gain_blocks[at, 0:1, :] for at in range(pairs)], axis=1)
    deep = x_ref.shape[1] // 8
    for at, ref in enumerate((wq_ref, wk_ref, wv_ref)):
        whole_weight(ref, qkv_ref, at * deep, deep)
    for ref in (dwq_ref, dwk_ref, dwv_ref, dgain_ref):
        ref[...] = jnp.zeros(ref.shape, f32)

    def gathered(ref, rows, factor):
        parts = [(ref[pair, rows, :] * factor).astype(bf16) for pair in range(pairs)]
        return jnp.concatenate(parts, axis=1)

    def common(rows):
        scaled, inverse = normalize(x_ref[rows, :].astype(f32))
        hidden_columns = (scaled * gain).astype(bf16).T
        key_grad = gathered(dk_ref, rows, LN2)
        value_grad = gathered(dv_ref, rows, 1.0)
        dwk_ref[...] += dot(hidden_columns, key_grad)
        dwv_ref[...] += dot(hidden_columns, value_grad)
        upstream = dot_nt(key_grad, wk_ref[...]) + dot_nt(value_grad, wv_ref[...])
        return scaled, inverse, hidden_columns, upstream

    def own_step(index, _):
        rows = block_at(index, BLOCK)
        scaled, inverse, hidden_columns, upstream = common(rows)
        parts = [dqt_ref[pair, :, rows].T for pair in range(pairs)]
        query_grad = jnp.concatenate(parts, axis=1)
        dwq_ref[...] += dot(hidden_columns, query_grad)
        upstream = upstream + dot_nt(query_grad, wq_ref[...])
        back, gain_sum = norm_back(upstream, scaled, inverse, gain)
        dgain_ref[0:1, :] += gain_sum
        own_ref[rows, :] = grad_self_ref[rows, :] + back
        return 0

    def other_step(index, _):
        rows = block_at(index + own // BLOCK, BLOCK)
        scaled, inverse, _, upstream = common(rows)
        back, gain_sum = norm_back(upstream, scaled, inverse, gain)
        dgain_ref[0:1, :] += gain_sum
        other_ref[block_at(index, BLOCK), :] = back.astype(bf16)
        return 0

    lax.fori_loop(0, own // BLOCK, own_step, 0)
    lax.fori_loop(0, x_ref.shape[0] // BLOCK - own // BLOCK, other_step, 0)


def call(kernel, outs, *operands, scratch=(), smem=0, params=PARAMS, spaces=None, out_space=VMEM):
    spaces = spaces or {}
    return pl.pallas_call(
        kernel,
        out_shape=[jax.ShapeDtypeStruct(shape, kind) for shape, kind in outs],
        in_specs=[
            pl.BlockSpec(memory_space=pltpu.SMEM if at < smem else spaces.get(at, VMEM))
            for at in range(len(operands))
        ],
        out_specs=[pl.BlockSpec(memory_space=out_space)] * len(outs),
        scratch_shapes=list(scratch),
        compiler_params=params,
    )(*operands)


def swapped(value, axis, bit):
    pairs = [(source, source ^ bit) for source in range(lax.axis_size(axis))]
    return lax.ppermute(value, axis, pairs)


def as_blocks(weight, chunks=1):
    height, width = weight.shape
    deep = height // 8
    cut = weight.reshape(4, 2, deep, 4, chunks, PAIR).transpose(3, 1, 0, 4, 2, 5)
    return cut.reshape(4, 2, 4, chunks * deep, PAIR)


def gather_plain(arguments, seq_size, dp_size):
    (decoder_in, source_states, out_grad, narrow, ffn_expand, ffn_reduce, gain_block) = arguments
    chip = lax.axis_index("seq") // 2
    rows_dec = decoder_in.shape[1]
    own = 2 * rows_dec
    outgoing = jnp.concatenate([decoder_in[1 - chip], source_states[1 - chip]], axis=0)
    arrived = swapped(outgoing, "seq", 2)
    own_rows = jnp.concatenate(
        [decoder_in[chip], arrived[:rows_dec], source_states[chip], arrived[rows_dec:]], axis=0
    )
    other_rows = swapped(own_rows, "seq", 1)
    x_all = jnp.concatenate([own_rows[:own], other_rows[:own]], axis=0)
    source_all = jnp.concatenate([own_rows[own:], other_rows[own:]], axis=0)
    cotangent = jnp.concatenate([out_grad[chip], swapped(out_grad[1 - chip], "seq", 2)], axis=0)

    def whole(weight):
        weight = lax.all_gather(weight, "seq", axis=1, tiled=True)
        return lax.all_gather(weight, "dp", axis=0, tiled=True)

    blocks = [as_blocks(whole(weight)) for weight in narrow]
    qkv = jnp.concatenate(blocks[:3], axis=3)
    later_a = jnp.concatenate(blocks[3:], axis=3)
    later_b = as_blocks(whole(ffn_expand), ffn_expand.shape[1] // PAIR)
    later_c = as_blocks(whole(ffn_reduce))
    gains = lax.all_gather(gain_block, "seq", axis=0)
    return x_all, source_all, cotangent, qkv, later_a, later_b, later_c, gains


def body(
    decoder_in,
    source_states,
    source_len,
    upsample,
    send_counts,
    self_query,
    self_key,
    self_value,
    self_output,
    cross_query,
    cross_key,
    cross_value,
    cross_output,
    ffn_expand,
    ffn_reduce,
    norm_gains,
    out_grad,
):
    both = ("dp", "seq")
    seq_size = lax.axis_size("seq")
    dp_size = lax.axis_size("dp")
    devices = dp_size * seq_size
    planes = dp_size // 2
    place = lax.axis_index("seq")
    chip = place // 2
    home_count, rows_dec, width = decoder_in.shape
    rows_src = source_states.shape[1]
    pairs = width // PAIR
    own = 2 * rows_dec
    total = 4 * rows_dec
    deep = self_query.shape[0]
    deep_two = ffn_reduce.shape[0]
    wide = ffn_expand.shape[1] // PAIR
    hidden_width = wide * PAIR * seq_size
    gain_block = jnp.pad(norm_gains.astype(f32), ((0, 5), (0, 0)))
    all_src = 4 * rows_src
    comm = dp_size == 8

    def pair_rows(rows):
        return (pairs, rows, PAIR)

    narrow = (self_query, self_key, self_value, self_output)
    narrow += (cross_query, cross_key, cross_value, cross_output)
    rows_outs = [
        (pair_rows(own), bf16),
        (pair_rows(total), bf16),
        (pair_rows(total), bf16),
        (pair_rows(own), bf16),
        ((pairs, 2, own, PAIR), bf16),
    ]
    buffers = [VMEM(shape, kind) for shape, kind in rows_outs]
    work = [
        VMEM((total, width), bf16),
        VMEM((width, 3 * PAIR), bf16),
        VMEM((total, PAIR), bf16),
        *buffers,
    ]
    semaphores = [pltpu.SemaphoreType.DMA((96,)), pltpu.SemaphoreType.DMA((96,))]
    if comm:
        cut = (seq_size, 2, planes)
        gathered = [
            ((total, width), bf16),
            ((all_src, width), bf16),
            ((own, width), bf16),
            (cut + (3 * deep, PAIR), bf16),
            (cut + (5 * deep, PAIR), bf16),
            (cut + (wide * deep, PAIR), bf16),
            (cut + (deep_two, PAIR), bf16),
            ((seq_size, 8, PAIR), f32),
        ]
        operands = (source_len, upsample, decoder_in, source_states, out_grad)
        operands += (*narrow, ffn_expand, ffn_reduce, gain_block)
        (
            x_all, source_all, cotangent, qkv, later_a, later_b, later_c, gains,
            q, k, v, mixed, query_extra,
        ) = call(
            partial(open_kernel, True, planes, deep),
            gathered + rows_outs,
            *operands,
            scratch=[
                VMEM((total, width), bf16),
                VMEM(cut + (3 * deep, PAIR), bf16),
                VMEM((seq_size, 8, PAIR), f32),
                *work,
                *semaphores,
            ],
            smem=2,
            spaces={at: pl.ANY for at in range(2, len(operands))},
            out_space=pl.ANY,
            params=pltpu.CompilerParams(
                vmem_limit_bytes=VMEM_LIMIT, collective_id=0, has_side_effects=True
            ),
        )
    else:
        x_all, source_all, cotangent, qkv, later_a, later_b, later_c, gains = gather_plain(
            (decoder_in, source_states, out_grad, narrow, ffn_expand, ffn_reduce, gain_block),
            seq_size,
            dp_size,
        )
        q, k, v, mixed, query_extra = call(
            partial(open_kernel, False, planes, deep),
            rows_outs,
            source_len,
            upsample,
            x_all,
            qkv,
            gains,
            scratch=[*work, *semaphores],
            smem=2,
            out_space=pl.ANY,
        )
    square = ((width, width), f32)
    (
        out_rows,
        grad_mixed,
        grad_self,
        dwo,
        dwcq,
        dwco,
        dw1,
        dw2t,
        dwck,
        dwcv,
        grad_source,
        dgain,
    ) = call(
        partial(middle_kernel, planes),
        [
            ((own, width), bf16),
            (pair_rows(own), bf16),
            ((own, width), f32),
            square,
            square,
            square,
            ((width, hidden_width), f32),
            ((width, hidden_width), f32),
            square,
            square,
            ((all_src, width), f32),
            ((8, width), f32),
        ],
        source_len,
        upsample,
        send_counts,
        x_all,
        mixed,
        cotangent,
        source_all,
        later_a,
        later_b,
        later_c,
        gains,
        scratch=[
            VMEM((own, width), bf16),
            *[VMEM((width, width), bf16)] * 5,
            VMEM((width, hidden_width), bf16),
            VMEM((hidden_width, width), bf16),
            VMEM(pair_rows(all_src), bf16),
            VMEM(pair_rows(all_src), bf16),
            VMEM((pairs, PAIR, all_src), bf16),
            VMEM((all_src, PAIR), bf16),
            VMEM(pair_rows(all_src), f32),
            VMEM(pair_rows(all_src), f32),
            pltpu.SemaphoreType.DMA,
            VMEM((pairs, BLOCK, PAIR), bf16),
            VMEM((2 * pairs, BLOCK, PAIR), bf16),
            VMEM((pairs, PAIR, BLOCK), bf16),
            VMEM((pairs, BLOCK, PAIR), bf16),
            VMEM((pairs, BLOCK, PAIR), bf16),
            VMEM((pairs, BLOCK, PAIR), bf16),
        ],
        smem=3,
        spaces={3: pl.ANY},
    )
    dqt, dk, dv = call(
        partial(self_back_kernel, planes),
        [
            ((pairs, PAIR, own), bf16),
            (pair_rows(total), f32),
            (pair_rows(total), f32),
        ],
        source_len,
        upsample,
        q,
        k,
        v,
        mixed,
        grad_mixed,
        query_extra,
        scratch=[VMEM((total, 2 * PAIR), bf16)] * 2 + [VMEM((PAIR, total), bf16)],
        smem=2,
    )
    own_grad, other_grad, dwq, dwk, dwv, dgain_one = call(
        partial(close_kernel, own),
        [
            ((own, width), f32),
            ((total - own, width), bf16),
            square,
            square,
            square,
            ((8, width), f32),
        ],
        x_all,
        qkv,
        gains,
        dqt,
        dk,
        dv,
        grad_self,
        scratch=[VMEM((width, width), bf16)] * 3,
    )

    half_src = all_src // 2
    crossing = jnp.concatenate([other_grad, grad_source[half_src:].astype(bf16)], axis=0)
    returned = swapped(crossing, "seq", 1).astype(f32)
    grad_rows = own_grad + returned[:own]
    source_rows = grad_source[:half_src] + returned[own:]
    homeward = jnp.concatenate(
        [out_rows[rows_dec:], grad_rows[rows_dec:].astype(bf16), source_rows[rows_src:].astype(bf16)],
        axis=0,
    )
    came = swapped(homeward, "seq", 2)

    def both_sentences(mine, theirs):
        return jnp.where(chip == 0, jnp.stack([mine, theirs]), jnp.stack([theirs, mine]))

    decoder_out = both_sentences(out_rows[:rows_dec], came[:rows_dec])
    grad_decoder = both_sentences(grad_rows[:rows_dec], came[rows_dec : 2 * rows_dec].astype(f32))
    grad_src = both_sentences(source_rows[:rows_src], came[2 * rows_dec :].astype(f32))

    def shares(grad, depth, columns):
        parts = grad.reshape(dp_size, depth, seq_size, columns).swapaxes(1, 2)
        return parts.reshape(dp_size, seq_size, depth * columns // PAIR, PAIR)

    dgains = jnp.stack([dgain_one[0], dgain[1], dgain[2]])
    dgains = jnp.concatenate([dgains, jnp.zeros((13, width), f32)], axis=0)
    dgains = dgains.reshape(1, 16, seq_size, PAIR).swapaxes(1, 2)
    dgains = jnp.broadcast_to(dgains, (dp_size, seq_size, 16, PAIR))
    dw2_parts = dw2t.reshape(seq_size, PAIR, dp_size, deep_two).transpose(2, 0, 1, 3)
    dw2_parts = dw2_parts.reshape(dp_size, seq_size, deep_two, PAIR)
    grads = [shares(grad, deep, PAIR) for grad in (dwq, dwk, dwv, dwo, dwcq, dwck, dwcv, dwco)]
    grads += [shares(dw1, deep, wide * PAIR), dw2_parts, dgains]
    grads = jnp.concatenate([grad.astype(bf16) for grad in grads], axis=2)
    total = lax.psum_scatter(
        grads.reshape(devices, -1, PAIR), both, scatter_dimension=0, tiled=True
    )[0].astype(f32)
    outs = [total[at * deep : (at + 1) * deep] for at in range(8)]
    start = 8 * deep
    outs.append(total[start : start + wide * deep].reshape(deep, wide * PAIR))
    start += wide * deep
    outs.append(total[start : start + deep_two].reshape(PAIR, deep_two).T)
    start += deep_two
    outs.append(total[start : start + 3])
    return (decoder_out, grad_decoder, grad_src, *outs)


def solution(mesh):
    rows = P("dp", "seq", None)
    weight = P("dp", "seq")
    placed = (rows, rows, P(), P(), P()) + (weight,) * 10 + (P(None, "seq"), rows)
    return jax.shard_map(
        body,
        mesh=mesh,
        in_specs=placed,
        out_specs=(rows, rows, rows) + (weight,) * 10 + (P(None, "seq"),),
        check_vma=False,
    )
```

time: 2320 us -> 461 us (0.20)
  matrix products: 768 us -> 0 us
  blocking collectives: 559 us -> 0 us
  waiting for transfers between devices: 517 us -> 144 us
  Pallas kernels: 0 us -> 234 us
  local copies, waits for them, and re-layouts: 262 us -> 43.5 us
  other arithmetic: 119 us -> 22.1 us
  starting transfers between devices: 55.7 us -> 1.9 us
    dot_general x198 -> x0, matrix products: 768 us -> none  [the longest x24 232 us: compute(): jnp.einsum('hqk,khd->qhd', score_low, key_rows, preferred_element_type=jn...]
    all_gather x19 -> x0, blocking collectives: 440 us -> none  [the longest x1 63.7 us: body(): lax.all_gather(columns[2], 'dp', axis=0, tiled=True)]
    pallas_call x0 -> x4, Pallas kernels: none -> 234 us  [call(): pl.pallas_call(kernel, out_shape=[jax.ShapeDtypeStruct(shape, kind) for s...]
    unnamed x33 -> x1, waiting for transfers between devices: 199 us -> 0.02 us
    reduce_scatter x11 -> x1, waiting for transfers between devices: 241 us -> 88.2 us  [body(): lax.psum_scatter(grads.reshape(devices, -1, PAIR), both, scatter_dimensio...]
    all_to_all x3 -> x0, blocking collectives: 84.7 us -> none  [the longest x1 28.3 us: body(): lax.all_to_all(from_heads(self_dv), 'seq', split_axis=1, concat_axis=2, t...]
    all_to_all x13 -> x0, waiting for transfers between devices: 76.5 us -> none  [the longest x1 22.9 us: body(): lax.all_to_all(from_heads(cross_dq), 'seq', split_axis=1, concat_axis=2,...]
    reshape x42 -> x3, local copies, waits for them, and re-layouts: 58.4 us -> 1.47 us  [the longest x2 0.79 us: body(): outs.append(total[start:start + deep_two].reshape(PAIR, deep_two).T)]
  transfers between devices with their start and end apart: 38 -> 3, of which waited for: 20 -> 3; matrix products, arithmetic and copies ran while one was open for 47% -> 2% of each run, Pallas kernels for 0% -> 0%
where the time goes in v1:
time: 461 us; the launch traced here: 460 us
  Pallas kernels  234 us (51%)
  waiting for transfers between devices  144 us (31%)
  local copies, waits for them, and re-layouts  43.5 us (9%)
  other arithmetic  22.1 us (5%)
  between operations  14.3 us (3%)
    pallas_call x4, Pallas kernels, call(): pl.pallas_call(kernel, out_shape=[jax.ShapeDtypeStruct(shape, kind) for s...  234 us
    reduce_scatter x1, waiting for transfers between devices, body(): lax.psum_scatter(grads.reshape(devices, -1, PAIR), both, scatter_dimensio...  88.2 us
    ppermute x2, waiting for transfers between devices, swapped(): return lax.ppermute(value, axis, pairs)  56 us
    convert_element_type x15, local copies, waits for them, and re-layouts, body(): grads = jnp.concatenate([grad.astype(bf16) for grad in grads], axis=2)  21.3 us
    unnamed x35, local copies, waits for them, and re-layouts  16 us
    convert_element_type x10, other arithmetic, body(): grads = jnp.concatenate([grad.astype(bf16) for grad in grads], axis=2)  11.8 us
  transfers between devices with their start and end apart: 3, of which 3 were waited for; matrix products, arithmetic and copies ran while one was open for 2% of the time, Pallas kernels for 0%

profile of v1, /device:TPU:0, one launch (start us, length us, event | category | flops | bytes accessed | tf_op | source)
XLA Modules:
  0.0 460.0 jit_solution(4217161146599512340)
XLA Ops:
  8.5 87.6 %shard_map.272 = (bf16[2048,512]{1,0:T(8,128)(2,1)}, bf16[512,512]{1,0:T(8,128)(2,1)}, bf16[1024,512]{1,0:T(8,128)(2,1)}, bf16[4,2,4,192,128]{4,3,2,1,0:T(8,128)...) custom-call(s32[16]{0:T(128)} %source_len_ref.5, ...), custom_call_target="tpu_custom_call" | custom-call | tf_op jit(solution)/shard_map/pallas_call | solution.py:893
  96.1 70.8 %shard_map.273 = (bf16[1024,512]{1,0:T(8,128)(2,1)}, bf16[4,1024,128]{2,1,0:T(8,128)(2,1)}, f32[1024,512]{1,0:T(8,128)}, f32[512,512]{1,0:T(8,128)}, f32[512,512...) custom-call(s32[16]{0:T(128)} %source_len_ref.5, ...), custom_call_target="tpu_custom_call" | custom-call | tf_op jit(solution)/shard_map/pallas_call | solution.py:893
  167.7 1.3 convert_element_type.132
  169.4 1.4 convert_element_type.138
  174.9 58.1 %shard_map.274 = (bf16[4,128,1024]{2,1,0:T(8,128)(2,1)}, f32[4,2048,128]{2,1,0:T(8,128)}, f32[4,2048,128]{2,1,0:T(8,128)}) custom-call(s32[16]{0:T(128)} %source_len_ref.5, s32[16]{0:T(128)} %upsample_ref.5, bf16[4,1024,128]{2,1,0:T(8,128)(2,1)} %get-tuple-element.58.q_ref, bf16[4,2048,128]{2,1,0:T(8,128)(2,1)} %get-tuple-element.59.k_ref, ...), custom_call_target="tpu_custom_call" | custom-call | tf_op jit(solution)/shard_map/pallas_call | solution.py:893
  233.0 17.4 %shard_map.275 = (f32[1024,512]{1,0:T(8,128)}, bf16[1024,512]{1,0:T(8,128)(2,1)}, f32[512,512]{1,0:T(8,128)}, f32[512,512]{1,0:T(8,128)}, f32[512,512]{1,0:T(8,128)}, /*index=5*/f32[8,512]{1,0:T(8,128)}) custom-call(bf16[2048,512]{1,0:T(8,128)(2,1)} %get-tuple-element.48.x_any.x_ref, bf16[4,2,4,192,128]{4,3,2,1,0:T(8,128)(2,1)} %get-tuple-element.57.qkv_ref, ...), custom_call_target="tpu_custom_call" | custom-call | tf_op jit(solution)/shard_map/pallas_call | solution.py:893
  251.3 1.4 convert_element_type.123
  256.8 2.5 convert_element_type.147
  259.3 2.8 convert_element_type.148
  262.1 3.5 copy.64
  265.5 3.4 convert_element_type.150
  268.9 2.5 convert_element_type.151
  272.1 1.8 copy.63
  273.9 4.2 convert_element_type.154
  278.0 2.1 bitcast_dynamic-update-slice_fusion.7
  280.1 2.0 bitcast_dynamic-update-slice_fusion.6
  287.9 1.7 constant_dynamic-update-slice_fusion.1
  290.1 1.7 constant_dynamic-update-slice_fusion
  294.8 2.6 collective-permute-done
  299.5 1.4 collective-permute-start.1
  301.0 53.4 %collective-permute-done.1 = bf16[1152,512]{1,0:T(8,128)(2,1)} collective-permute-done((bf16[1152,512]{1,0:T(8,128)(2,1)}, bf16[1152,512]{1,0:T(8,128)(2,1)}, u32[]{:S(2)}, u32[]{:S(2)}) %collective-permute-start.1) | collective-permute-done | bytes 1179680 | tf_op jit(solution)/shard_map/ppermute | solution.py:908
  356.2 1.4 fusion
  358.7 1.5 maximum_select_fusion
  360.2 88.2 %reduce-scatter.2.cloned.1.call-done = bf16[1,1040,128]{2,1,0:T(8,128)(2,1)} async-done(((bf16[32,1040,128]{2,1,0:T(8,128)(2,1)}), bf16[1,1040,128]{2,1,0:T(8,128)(2,1)}) %reduce-scatter.2.cloned.1.call-update) | async-done | bytes 266256 | tf_op jit(solution)/shard_map/reduce_scatter | solution.py:1190
  (77 shorter events, 31.1 us)
Async XLA Ops:
  7.2 441.3 %reduce-scatter.2.cloned.1.call-start = ((), (), s32[]{:S(2)}) async-start(), calls=%async_computation.1 | async-start | bytes 8785920 | tf_op jit(solution)/shard_map/reduce_scatter | solution.py:1190
  166.9 2.2 copy-start.8
  169.4 4.5 copy-start.7
  251.3 4.5 copy-start.6
  278.0 4.1 copy-start.5
  280.1 4.9 %copy-start.2 = (bf16[8,64,4,128]{3,2,1,0:T(4,128)(2,1)S(1)}, bf16[8,64,4,128]{3,2,1,0:T(4,128)(2,1)}, u32[]{:S(2)}) copy-start(bf16[8,64,4,128]{3,2,1,0:T(4,128)(2,1)} %convert_element_type.139) | copy-start | bytes 1572868
  282.1 3.8 copy-start.3
  283.1 3.8 copy-start.4
  287.9 2.2 copy-start
  292.6 1.2 copy-start.11
  292.6 1.5 copy-start.10
  292.6 2.1 copy-start.9
  294.2 3.2 collective-permute-start
  294.8 3.1 copy-start.1
  299.5 54.9 %collective-permute-start.1 = (bf16[1152,512]{1,0:T(8,128)(2,1)}, bf16[1152,512]{1,0:T(8,128)(2,1)}, u32[]{:S(2)}, u32[]{:S(2)}) collective-permute-start(bf16[1152,512]{1,0:T(8,128)(2,1)} %pad_maximum_fusion.1), channel_id=1, source_target_pairs={{0,2},{1,3},{2,0},{3,1},{4,6},{5,7},{6,4},{7,5},{8,10},{9,11},{10,... | collective-permute-start | bytes 3538952 | tf_op jit(solution)/shard_map/ppermute | solution.py:908
Sparse Core Ops, SparseCore 0:
  292.7 155.7 reduce-scatter.1

commit v2 on v1

--- a/solution.py
+++ b/solution.py
@@ -530,6 +530,19 @@
                     ]
 
 
+def to_blocks(blocks, start, count, ref, chunks=1):
+    columns, sides, planes = blocks.shape[:3]
+    for column in range(columns):
+        for side in range(sides):
+            for plane in range(planes):
+                row = (plane * sides + side) * count
+                for chunk in range(chunks):
+                    at = (column * chunks + chunk) * PAIR
+                    blocks[
+                        column, side, plane, start + chunk * count : start + (chunk + 1) * count, :
+                    ] = ref[row : row + count, at : at + PAIR].astype(bf16)
+
+
 def middle_kernel(
     planes,
     source_len_ref,
@@ -546,6 +559,11 @@
     out_ref,
     grad_mixed_ref,
     grad_self_ref,
+    part_a,
+    part_b,
+    part_c,
+    grad_source_ref,
+    dgain_ref,
     dwo_ref,
     dwcq_ref,
     dwco_ref,
@@ -553,8 +571,6 @@
     dw2t_ref,
     dwck_ref,
     dwcv_ref,
-    grad_source_ref,
-    dgain_ref,
     x_ref,
     wo_ref,
     wcq_ref,
@@ -746,150 +762,505 @@
         value_grad = gathered(dcv_ref, rows, 1.0)
         dwck_ref[...] += dot(source_columns, key_grad)
         dwcv_ref[...] += dot(source_columns, value_grad)
-        grad_source_ref[rows, :] = dot_nt(key_grad, wck_ref[...]) + dot_nt(
-            value_grad, wcv_ref[...]
+        grad_source_ref[rows, :] = (
+            dot_nt(key_grad, wck_ref[...]) + dot_nt(value_grad, wcv_ref[...])
+        ).astype(bf16)
+        return 0
+
+    lax.fori_loop(0, few // BLOCK, source_back, 0)
+    for at, ref in enumerate((dwo_ref, dwcq_ref, dwck_ref, dwcv_ref, dwco_ref)):
+        to_blocks(part_a, at * deep, deep, ref)
+    to_blocks(part_b, 0, deep, dw1_ref, hidden_width // width)
+    deep_two = hidden_width // 8
+    for column in range(4):
+        for side in range(2):
+            for plane in range(4):
+                for half in range(2):
+                    at = (plane * 2 + side) * deep_two + half * PAIR
+                    part_c[column, side, plane, half * PAIR : (half + 1) * PAIR, :] = dw2t_ref[
+                        column * PAIR : (column + 1) * PAIR, at : at + PAIR
+                    ].astype(bf16)
+
+
+def last_kernel(comm, planes, source_len_ref, upsample_ref, *refs):
+    (q_any, k_any, v_any, mixed_any, grad_any, extra_any) = refs[:6]
+    (x_any, qkv_any, gain_any, grad_self_any, dgain_any) = refs[6:11]
+    refs = refs[11:]
+    if comm:
+        (part_a, part_b, part_c, source_any, rows_any) = refs[:5]
+        (decoder_out, grad_out, source_out, *weight_outs, gain_out) = refs[5:19]
+        refs = refs[19:]
+    else:
+        (own_out, other_out, part_out, gain_out) = refs[:4]
+        refs = refs[4:]
+    (
+        q_s, k_s, v_s, mixed_s, grad_s, extra_s, x_s, qkv_s, gain_s, grad_self_s, dgain_s,
+        dk_s, dv_s, keys_s, values_s, kt_s, hidden_s, total_s, dkv_s, dq_s, weight_s,
+        part_s, load, send, receive,
+    ) = refs[:25]
+    refs = refs[25:]
+    where = Where(planes)
+    chip, core, side, plane = where.chip, where.core, where.side, where.plane
+    total, width = x_s.shape
+    own = total // 2
+    rows = total // 4
+    pairs = width // PAIR
+    deep = width // 8
+    chunk = 512
+    size = 512
+    blocks = own // size
+    lane = lax.broadcasted_iota(jnp.int32, (size, PAIR), 1)
+    semaphores = Semaphores(send, receive)
+    sentence = where.group * 2 + chip
+    length = source_len_ref[sentence] * upsample_ref[sentence]
+
+    def turn_pair(turn):
+        return where.column(pairs - 1 - turn)
+
+    def turn_loads(turn):
+        pair, slot = turn_pair(turn), turn % 2
+        return [
+            pltpu.make_async_copy(source.at[pair], target.at[slot], load.at[slot, at])
+            for at, (source, target) in enumerate(
+                (
+                    (q_any, q_s),
+                    (k_any, k_s),
+                    (v_any, v_s),
+                    (mixed_any, mixed_s),
+                    (grad_any, grad_s),
+                    (extra_any, extra_s),
+                )
+            )
+        ]
+
+    for copy in turn_loads(0):
+        copy.start()
+    common = [
+        semaphores.local(source, target)
+        for source, target in (
+            (x_any, x_s),
+            (qkv_any, qkv_s),
+            (gain_any, gain_s),
+            (dgain_any, dgain_s),
+            (grad_self_any, grad_self_s),
         )
+    ]
+    for copy in common:
+        copy.start()
+
+    def begin(copies):
+        for copy in copies:
+            copy.start()
+
+    def arrive(copies):
+        for copy in copies:
+            copy.wait_recv()
+
+    if comm:
+        (
+            keep_a, keep_b, keep_c, core_a, core_b, core_c, far_a, far_b, far_c,
+            near_a, near_b, near_c, planes_a, planes_b, planes_c,
+            land_q, far_q, planes_q, gain_send, gain_land, gain_far, gain_planes, grads_send,
+            grads_land, cross_send, cross_land, stage, source_s, source_land, source_far, stage_s,
+        ) = refs
+        place, across = where.place, where.column(2)
+        pieces = []
+        for part, keep, land, far, near, land_planes, side_first in (
+            (part_a, keep_a, core_a, far_a, near_a, planes_a, True),
+            (part_b, keep_b, core_b, far_b, near_b, planes_b, False),
+            (part_c, keep_c, core_c, far_c, near_c, planes_c, True),
+        ):
+            piece = dict(keep=keep, land=land, far=far, near=near, planes=land_planes)
+            piece["load"] = [
+                semaphores.local(part.at[place], keep.at[0]),
+                semaphores.local(part.at[across], keep.at[1]),
+            ]
+            piece["core"] = [
+                semaphores.remote(part.at[where.column(1)], land.at[0], where.other_core),
+                semaphores.remote(part.at[where.column(3)], land.at[1], where.other_core),
+            ]
+            if side_first:
+                piece["far"] = [
+                    semaphores.remote(keep.at[at, 1 - side], far.at[at], where.other_side)
+                    for at in (0, 1)
+                ]
+                piece["near"] = [semaphores.remote(keep.at[1, side], near, where.other_chip)]
+            else:
+                piece["far"] = [
+                    semaphores.remote(keep.at[1, at], far.at[at], where.other_chip)
+                    for at in (0, 1)
+                ]
+                piece["near"] = [semaphores.remote(keep.at[0, 1 - side], near, where.other_side)]
+            piece["last"] = [
+                semaphores.remote(
+                    keep.at[0, side, (plane + step) % planes],
+                    land_planes.at[step - 1],
+                    where.other_planes[step - 1],
+                )
+                for step in range(1, planes)
+            ]
+            piece["side_first"] = side_first
+            pieces.append(piece)
+        a, b, c = pieces
+        owners = (where.diagonal, where.other_chip, where.other_core)
+        send_q = [
+            semaphores.remote(part_s.at[turn], land_q.at[turn], owners[turn]) for turn in range(3)
+        ]
+        side_q = semaphores.remote(part_s.at[3, 1 - side], far_q, where.other_side)
+        plane_q = [
+            semaphores.remote(
+                part_s.at[3, side, (plane + step) % planes],
+                planes_q.at[step - 1],
+                where.other_planes[step - 1],
+            )
+            for step in range(1, planes)
+        ]
+        gain_group = [
+            semaphores.remote(gain_send.at[where.column(3 - turn)], gain_land.at[turn], owners[turn])
+            for turn in range(3)
+        ]
+        gain_side = semaphores.remote(gain_land.at[3], gain_far, where.other_side)
+        gain_last = [
+            semaphores.remote(
+                gain_planes.at[plane], gain_planes.at[plane], where.other_planes[step - 1]
+            )
+            for step in range(1, planes)
+        ]
+        rows_local = semaphores.local(rows_any.at[:rows], decoder_out.at[chip])
+        rows_cross = semaphores.remote(rows_any.at[rows:], decoder_out.at[chip], where.other_chip)
+        few = source_any.shape[0] // 4
+        source_local = semaphores.local(source_any.at[: 2 * few], source_s)
+        source_core = semaphores.remote(source_any.at[2 * few :], source_land, where.other_core)
+        source_cross = semaphores.remote(source_s.at[few:], source_far, where.other_chip)
+        grads_core = [
+            semaphores.remote(grads_send.at[at], grads_land.at[at], where.other_core)
+            for at in range(2)
+        ]
+        grads_cross = [
+            semaphores.remote(cross_send.at[at], cross_land.at[at], where.other_chip)
+            for at in range(rows // BLOCK)
+        ]
+        stage_out = [
+            semaphores.local(stage.at[at], grad_out.at[chip if at == 0 else 1 - chip])
+            for at in range(2)
+        ]
+        source_outs = [
+            semaphores.local(stage_s.at[at], source_out.at[chip if at == 0 else 1 - chip])
+            for at in range(2)
+        ]
+        for piece in pieces:
+            begin(piece["load"])
+        begin([rows_local, source_local])
+        entry_barrier(where.everyone())
+        for piece in pieces:
+            begin(piece["core"])
+        begin([source_core, rows_cross])
+
+        def add_in(ref, land):
+            def add(at, _):
+                ref[at] = (ref[at].astype(f32) + land[at].astype(f32)).astype(bf16)
+                return 0
+
+            lax.fori_loop(0, planes, add, 0)
+
+        def add_core(piece):
+            for copy in piece["load"]:
+                copy.wait()
+            arrive(piece["core"])
+            for at in (0, 1):
+                for half in (0, 1):
+                    add_in(piece["keep"].at[at, half], piece["land"].at[at, half])
+            begin(piece["far"])
+
+        def add_far(piece):
+            arrive(piece["far"])
+            for at in (0, 1):
+                if piece["side_first"]:
+                    add_in(piece["keep"].at[at, side], piece["far_land"].at[at])
+                else:
+                    add_in(piece["keep"].at[0, at], piece["far_land"].at[at])
+            begin(piece["near"])
+
+        def add_near(piece):
+            arrive(piece["near"])
+            add_in(piece["keep"].at[0, side], piece["near_land"])
+            begin(piece["last"])
+
+        def finish(piece):
+            arrive(piece["last"])
+            value = piece["keep"][0, side, plane].astype(f32)
+            for step in range(planes - 1):
+                value = value + piece["planes"][step].astype(f32)
+            return value
+
+        for piece, far, near in ((a, far_a, near_a), (b, far_b, near_b), (c, far_c, near_c)):
+            piece["far_land"], piece["near_land"] = far, near
+
+    mask_columns(chip, core, rows, total, BLOCK, length, values_s.at[:, PAIR:])
+    keys_s[:, PAIR:] = values_s[:, PAIR:]
+    for copy in common:
+        copy.wait()
+    gain = jnp.concatenate([gain_s[at, 0:1, :] for at in range(pairs)], axis=1)
+
+    def hide(index, _):
+        at = block_at(index, BLOCK)
+        scaled, _ = normalize(x_s[at, :].astype(f32))
+        hidden_s[:, at] = (scaled * gain).astype(bf16).T
         return 0
 
-    lax.fori_loop(0, few // BLOCK, source_back, 0)
-
-
-def self_back_kernel(
-    planes,
-    source_len_ref,
-    upsample_ref,
-    q_ref,
-    k_ref,
-    v_ref,
-    mixed_ref,
-    grad_ref,
-    query_extra_ref,
-    dqt_ref,
-    dk_ref,
-    dv_ref,
-    keys_s,
-    values_s,
-    kt_s,
-):
-    pairs, rows_own, _ = q_ref.shape
-    keys = k_ref.shape[1]
-    where = Where(planes)
-    sentence = where.group * 2 + where.chip
-    length = source_len_ref[sentence] * upsample_ref[sentence]
-    extra = values_s.at[:, PAIR:]
-    mask_columns(where.chip, where.core, keys // 4, keys, BLOCK, length, extra)
-    keys_s[:, PAIR:] = values_s[:, PAIR:]
-    size = 2 * BLOCK
-    blocks = rows_own // size
-    lane = lax.broadcasted_iota(jnp.int32, (size, PAIR), 1)
-    chunk = 512
+    lax.fori_loop(0, total // BLOCK, hide, 0)
+
+    def take_weights(turn, pair):
+        for part in range(3):
+            for at in range(8):
+                weight_s[turn, at * 64 : at * 64 + 64, part * PAIR : (part + 1) * PAIR] = qkv_s[
+                    pair, at % 2, at // 2, part * 64 : part * 64 + 64, :
+                ]
+
+    def upstream(turns, at, own_rows):
+        value = None
+        for turn in turns:
+            term = dot_nt(dkv_s[turn, at, :], weight_s[turn, :, PAIR:])
+            if own_rows:
+                term = term + dot_nt(dq_s[turn, at, :], weight_s[turn, :, :PAIR])
+            value = term if value is None else value + term
+        return value
 
     def step(index, _):
-        pair = index // blocks
-        rows = block_at(index % blocks, size)
+        turn = index // blocks
+        pair, slot = turn_pair(turn), turn % 2
+        at = block_at(index % blocks, size)
+        if comm:
+
+            @pl.when(index == 1)
+            def _():
+                add_core(a)
+                add_core(b)
+                source_local.wait()
+                arrive([source_core])
+                for half in range(2):
+                    r = slice(half * few, (half + 1) * few)
+                    value = source_s[r, :].astype(f32) + source_land[r, :].astype(f32)
+                    source_s[r, :] = value.astype(bf16)
+                    if half == 0:
+                        stage_s[0] = value
+                begin([source_cross, source_outs[0]])
+
+            @pl.when(index == 3)
+            def _():
+                add_far(a)
+                add_core(c)
+
+            @pl.when(index == 4)
+            def _():
+                add_far(b)
+
+            @pl.when(index == 5)
+            def _():
+                add_near(a)
+                add_far(c)
+
+            @pl.when(index == 6)
+            def _():
+                add_near(b)
+
+            @pl.when(index == 7)
+            def _():
+                add_near(c)
 
         @pl.when(index % blocks == 0)
         def _():
-            dk_ref[pair] = jnp.zeros((keys, PAIR), f32)
-            dv_ref[pair] = jnp.zeros((keys, PAIR), f32)
-            keys_s[:, :PAIR] = k_ref[pair]
-            values_s[:, :PAIR] = v_ref[pair]
-            kt_s[...] = k_ref[pair].T
+            for copy in turn_loads(turn):
+                copy.wait()
+
+            @pl.when(turn + 1 < pairs)
+            def _():
+                for copy in turn_loads(turn + 1):
+                    copy.start()
+
+            dk_s[...] = jnp.zeros(dk_s.shape, f32)
+            dv_s[...] = jnp.zeros(dv_s.shape, f32)
+            keys_s[:, :PAIR] = k_s[slot]
+            values_s[:, :PAIR] = v_s[slot]
+            kt_s[...] = k_s[slot].T
+            take_weights(turn, pair)
 
         def part(ref):
-            return lambda at: ref[at * chunk : (at + 1) * chunk, :]
+            return lambda part: ref[part * chunk : (part + 1) * chunk, :]
 
         def add_to(ref):
-            def add(at, value):
-                ref[pair, at * chunk : (at + 1) * chunk, :] += value
+            def add(part, value):
+                ref[part * chunk : (part + 1) * chunk, :] += value
 
             return add
 
-        dqt_ref[pair, :, rows] = attend_pair_back(
-            q_ref[pair, rows, :],
-            grad_ref[pair, rows, :],
-            mixed_ref[pair, rows, :],
-            [query_extra_ref[pair, head, rows, :] for head in (0, 1)],
+        query_grad = attend_pair_back(
+            q_s[slot, at, :],
+            grad_s[slot, at, :],
+            mixed_s[slot, at, :],
+            [extra_s[slot, head, at, :] for head in (0, 1)],
             part(keys_s),
             part(values_s),
-            lambda at, head: kt_s[64 * head : 64 * head + 64, at * chunk : (at + 1) * chunk],
-            keys // chunk,
+            lambda part, head: kt_s[64 * head : 64 * head + 64, part * chunk : (part + 1) * chunk],
+            total // chunk,
             lane,
-            add_to(dk_ref),
-            add_to(dv_ref),
+            add_to(dk_s),
+            add_to(dv_s),
         )
+        dq_s[turn, at, :] = query_grad.T
+
+        @pl.when(index % blocks == blocks - 1)
+        def _():
+            dkv_s[turn, :, :PAIR] = (dk_s[...] * LN2).astype(bf16)
+            dkv_s[turn, :, PAIR:] = dv_s[...].astype(bf16)
+            both = dot(hidden_s[...], dkv_s[turn]).astype(bf16)
+            query = dot(hidden_s[:, :own], dq_s[turn]).astype(bf16)
+            for at in range(8):
+                r = slice(at * deep, (at + 1) * deep)
+                for part, value in enumerate(
+                    (query[r, :], both[r, :PAIR], both[r, PAIR:])
+                ):
+                    part_s[turn, at % 2, at // 2, part * deep : (part + 1) * deep, :] = value
+
+        if comm:
+            for sent in range(3):
+
+                @pl.when(index == sent * blocks + blocks - 1)
+                def _():
+                    send_q[sent].start()
+
+        @pl.when(index == (pairs - 1) * blocks - 1)
+        def _():
+            def early(row, _):
+                r = block_at(row, BLOCK)
+                total_s[r, :] = upstream(range(pairs - 1), r, True)
+                return 0
+
+            def early_other(row, _):
+                r = block_at(row, BLOCK)
+                total_s[r, :] = upstream(range(pairs - 1), r, False)
+                return 0
+
+            lax.fori_loop(0, own // BLOCK, early, 0)
+            lax.fori_loop(own // BLOCK, total // BLOCK, early_other, 0)
+
         return 0
 
     lax.fori_loop(0, pairs * blocks, step, 0)
 
-
-def close_kernel(
-    own,
-    x_ref,
-    qkv_ref,
-    gain_blocks,
-    dqt_ref,
-    dk_ref,
-    dv_ref,
-    grad_self_ref,
-    own_ref,
-    other_ref,
-    dwq_ref,
-    dwk_ref,
-    dwv_ref,
-    dgain_ref,
-    wq_ref,
-    wk_ref,
-    wv_ref,
-):
-    pairs = dk_ref.shape[0]
-    gain = jnp.concatenate([gain_blocks[at, 0:1, :] for at in range(pairs)], axis=1)
-    deep = x_ref.shape[1] // 8
-    for at, ref in enumerate((wq_ref, wk_ref, wv_ref)):
-        whole_weight(ref, qkv_ref, at * deep, deep)
-    for ref in (dwq_ref, dwk_ref, dwv_ref, dgain_ref):
-        ref[...] = jnp.zeros(ref.shape, f32)
-
-    def gathered(ref, rows, factor):
-        parts = [(ref[pair, rows, :] * factor).astype(bf16) for pair in range(pairs)]
-        return jnp.concatenate(parts, axis=1)
-
-    def common(rows):
-        scaled, inverse = normalize(x_ref[rows, :].astype(f32))
-        hidden_columns = (scaled * gain).astype(bf16).T
-        key_grad = gathered(dk_ref, rows, LN2)
-        value_grad = gathered(dv_ref, rows, 1.0)
-        dwk_ref[...] += dot(hidden_columns, key_grad)
-        dwv_ref[...] += dot(hidden_columns, value_grad)
-        upstream = dot_nt(key_grad, wk_ref[...]) + dot_nt(value_grad, wv_ref[...])
-        return scaled, inverse, hidden_columns, upstream
-
-    def own_step(index, _):
-        rows = block_at(index, BLOCK)
-        scaled, inverse, hidden_columns, upstream = common(rows)
-        parts = [dqt_ref[pair, :, rows].T for pair in range(pairs)]
-        query_grad = jnp.concatenate(parts, axis=1)
-        dwq_ref[...] += dot(hidden_columns, query_grad)
-        upstream = upstream + dot_nt(query_grad, wq_ref[...])
-        back, gain_sum = norm_back(upstream, scaled, inverse, gain)
-        dgain_ref[0:1, :] += gain_sum
-        own_ref[rows, :] = grad_self_ref[rows, :] + back
+    def row_back(row, own_rows):
+        r = block_at(row, BLOCK)
+        scaled, inverse = normalize(x_s[r, :].astype(f32))
+        value = total_s[r, :] + upstream([pairs - 1], r, own_rows)
+        back, gain_sum = norm_back(value, scaled, inverse, gain)
+        dgain_s[0:1, :] += gain_sum
+        return r, back
+
+    per = rows // BLOCK
+    if not comm:
+
+        def own_step(row, _):
+            r, back = row_back(row, True)
+            grad_self_s[r, :] += back
+            return 0
+
+        def other_step(row, _):
+            r, back = row_back(row, False)
+            total_s[r, :] = back
+            return 0
+
+        lax.fori_loop(0, 2 * per, own_step, 0)
+        lax.fori_loop(2 * per, 4 * per, other_step, 0)
+        own_out[...] = grad_self_s[...]
+        other_out[...] = total_s[own:, :].astype(bf16)
+        for turn in range(pairs):
+            part_out[turn_pair(turn)] = part_s[turn]
+        gain_out[...] = dgain_s[...]
+        return
+
+    def add_q(at, _):
+        for half in range(2):
+            value = part_s[3, half, at].astype(f32)
+            for turn in range(3):
+                value = value + land_q[turn, half, at].astype(f32)
+            part_s[3, half, at] = value.astype(bf16)
         return 0
 
-    def other_step(index, _):
-        rows = block_at(index + own // BLOCK, BLOCK)
-        scaled, inverse, _, upstream = common(rows)
-        back, gain_sum = norm_back(upstream, scaled, inverse, gain)
-        dgain_ref[0:1, :] += gain_sum
-        other_ref[block_at(index, BLOCK), :] = back.astype(bf16)
-        return 0
-
-    lax.fori_loop(0, own // BLOCK, own_step, 0)
-    lax.fori_loop(0, x_ref.shape[0] // BLOCK - own // BLOCK, other_step, 0)
-
-
-def call(kernel, outs, *operands, scratch=(), smem=0, params=PARAMS, spaces=None, out_space=VMEM):
+    def other_rows(slot):
+        def other_step(row, _):
+            _, back = row_back(slot * per + row, False)
+            grads_send[slot - 2, block_at(row, BLOCK), :] = back.astype(bf16)
+            return 0
+
+        lax.fori_loop(0, per, other_step, 0)
+        grads_core[slot - 2].start()
+
+    other_rows(3)
+    arrive(send_q)
+    lax.fori_loop(0, planes, add_q, 0)
+    side_q.start()
+    other_rows(2)
+    arrive([grads_core[1]])
+    for row in range(per):
+        r, back = row_back(per + row, True)
+        value = back + grad_self_s[r, :] + grads_land[1, row * BLOCK : (row + 1) * BLOCK, :].astype(f32)
+        cross_send[row] = value.astype(bf16)
+        grads_cross[row].start()
+    arrive([side_q])
+    add_in(part_s.at[3, side], far_q)
+    begin(plane_q)
+    arrive([grads_core[0]])
+    for row in range(per):
+        r, back = row_back(row, True)
+        r_own = slice(row * BLOCK, (row + 1) * BLOCK)
+        stage[0, r_own, :] = back + grad_self_s[r, :] + grads_land[0, r_own, :].astype(f32)
+    stage_out[0].start()
+
+    for at in range(pairs):
+        gain_send[at] = dgain_s[:, at * PAIR : (at + 1) * PAIR]
+    begin(gain_group)
+    sums = [finish(piece) for piece in pieces]
+    arrive(gain_group)
+    gain_land[3] = gain_send[place] + gain_land[0] + gain_land[1] + gain_land[2]
+    gain_side.start()
+    for at in range(5):
+        weight_outs[3 + at][...] = sums[0][at * deep : (at + 1) * deep, :]
+    for at in range(sums[1].shape[0] // deep):
+        weight_outs[8][:, at * PAIR : (at + 1) * PAIR] = sums[1][at * deep : (at + 1) * deep, :]
+    for at in range(sums[2].shape[0] // PAIR):
+        r = slice(at * PAIR, (at + 1) * PAIR)
+        weight_outs[9][r, :] = sums[2][r, :].T
+    arrive([source_cross])
+    stage_s[1] = source_far[...].astype(f32)
+    source_outs[1].start()
+    arrive([gain_side])
+    gain_planes[plane] = gain_land[3] + gain_far[...]
+    begin(gain_last)
+    arrive(plane_q)
+    value = part_s[3, side, plane].astype(f32)
+    for at in range(planes - 1):
+        value = value + planes_q[at].astype(f32)
+    for at in range(3):
+        weight_outs[at][...] = value[at * deep : (at + 1) * deep, :]
+    for row in range(per):
+        arrive([grads_cross[row]])
+        stage[1, row * BLOCK : (row + 1) * BLOCK, :] = cross_land[row].astype(f32)
+    stage_out[1].start()
+    arrive(gain_last)
+    value = gain_planes[0]
+    for at in range(1, planes):
+        value = value + gain_planes[at]
+    gain_out[...] = value
+    arrive([rows_cross])
+    for copy in [rows_local, *stage_out, *source_outs]:
+        copy.wait()
+    for copy in semaphores.sent:
+        copy.wait_send()
+
+
+def call(kernel, outs, *operands, scratch=(), smem=0, params=PARAMS, spaces=None, out_space=VMEM, out_spaces=None):
     spaces = spaces or {}
+    out_spaces = out_spaces or {}
     return pl.pallas_call(
         kernel,
         out_shape=[jax.ShapeDtypeStruct(shape, kind) for shape, kind in outs],
@@ -897,7 +1268,9 @@
             pl.BlockSpec(memory_space=pltpu.SMEM if at < smem else spaces.get(at, VMEM))
             for at in range(len(operands))
         ],
-        out_specs=[pl.BlockSpec(memory_space=out_space)] * len(outs),
+        out_specs=[
+            pl.BlockSpec(memory_space=out_spaces.get(at, out_space)) for at in range(len(outs))
+        ],
         scratch_shapes=list(scratch),
         compiler_params=params,
     )(*operands)
@@ -913,6 +1286,12 @@
     deep = height // 8
     cut = weight.reshape(4, 2, deep, 4, chunks, PAIR).transpose(3, 1, 0, 4, 2, 5)
     return cut.reshape(4, 2, 4, chunks * deep, PAIR)
+
+
+def from_blocks(blocks, chunks=1):
+    height = blocks.shape[3] // chunks
+    cut = blocks.reshape(4, 2, 4, chunks, height, PAIR).transpose(2, 1, 4, 0, 3, 5)
+    return cut.reshape(8 * height, 4 * chunks * PAIR)
 
 
 def gather_plain(arguments, seq_size, dp_size):
@@ -962,10 +1341,8 @@
     norm_gains,
     out_grad,
 ):
-    both = ("dp", "seq")
     seq_size = lax.axis_size("seq")
     dp_size = lax.axis_size("dp")
-    devices = dp_size * seq_size
     planes = dp_size // 2
     place = lax.axis_index("seq")
     chip = place // 2
@@ -1055,34 +1432,20 @@
             smem=2,
             out_space=pl.ANY,
         )
-    square = ((width, width), f32)
-    (
-        out_rows,
-        grad_mixed,
-        grad_self,
-        dwo,
-        dwcq,
-        dwco,
-        dw1,
-        dw2t,
-        dwck,
-        dwcv,
-        grad_source,
-        dgain,
-    ) = call(
+    square = VMEM((width, width), f32)
+    parts = [
+        ((seq_size, 2, 4, 5 * width // 8, PAIR), bf16),
+        ((seq_size, 2, 4, hidden_width // 8, PAIR), bf16),
+        ((seq_size, 2, 4, hidden_width // 8, PAIR), bf16),
+    ]
+    out_rows, grad_mixed, grad_self, part_a, part_b, part_c, grad_source, dgain = call(
         partial(middle_kernel, planes),
         [
             ((own, width), bf16),
             (pair_rows(own), bf16),
             ((own, width), f32),
-            square,
-            square,
-            square,
-            ((width, hidden_width), f32),
-            ((width, hidden_width), f32),
-            square,
-            square,
-            ((all_src, width), f32),
+            *parts,
+            ((all_src, width), bf16),
             ((8, width), f32),
         ],
         source_len,
@@ -1097,6 +1460,9 @@
         later_c,
         gains,
         scratch=[
+            *[square] * 3,
+            *[VMEM((width, hidden_width), f32)] * 2,
+            *[square] * 2,
             VMEM((own, width), bf16),
             *[VMEM((width, width), bf16)] * 5,
             VMEM((width, hidden_width), bf16),
@@ -1118,86 +1484,146 @@
         smem=3,
         spaces={3: pl.ANY},
     )
-    dqt, dk, dv = call(
-        partial(self_back_kernel, planes),
-        [
-            ((pairs, PAIR, own), bf16),
-            (pair_rows(total), f32),
-            (pair_rows(total), f32),
-        ],
-        source_len,
-        upsample,
-        q,
-        k,
-        v,
-        mixed,
-        grad_mixed,
-        query_extra,
-        scratch=[VMEM((total, 2 * PAIR), bf16)] * 2 + [VMEM((PAIR, total), bf16)],
-        smem=2,
+    part_q = ((seq_size, 2, 4, 3 * width // 8, PAIR), bf16)
+    operands = (source_len, upsample, q, k, v, mixed, grad_mixed, query_extra)
+    operands += (x_all, qkv, gains, grad_self, dgain)
+    work = [
+        VMEM((2, own, PAIR), bf16),
+        VMEM((2, total, PAIR), bf16),
+        VMEM((2, total, PAIR), bf16),
+        VMEM((2, own, PAIR), bf16),
+        VMEM((2, own, PAIR), bf16),
+        VMEM((2, 2, own, PAIR), bf16),
+        VMEM((total, width), bf16),
+        VMEM(qkv.shape, bf16),
+        VMEM(gains.shape, f32),
+        VMEM((own, width), f32),
+        VMEM((8, width), f32),
+        VMEM((total, PAIR), f32),
+        VMEM((total, PAIR), f32),
+        VMEM((total, 2 * PAIR), bf16),
+        VMEM((total, 2 * PAIR), bf16),
+        VMEM((PAIR, total), bf16),
+        VMEM((width, total), bf16),
+        VMEM((total, width), f32),
+        VMEM((pairs, total, 2 * PAIR), bf16),
+        VMEM((pairs, own, PAIR), bf16),
+        VMEM((pairs, width, 3 * PAIR), bf16),
+        VMEM(*part_q),
+        pltpu.SemaphoreType.DMA((2, 6)),
+        *semaphores,
+    ]
+    everywhere = {at: pl.ANY for at in range(2, 18)}
+    if comm:
+        heights = [shape[3] for shape, _ in parts]
+
+        def per_piece(lead):
+            return [VMEM((*lead, height, PAIR), bf16) for height in heights]
+
+        work += [
+            *per_piece((2, 2, planes)),
+            *per_piece((2, 2, planes)),
+            *per_piece((2, planes)),
+            *per_piece((planes,)),
+            *per_piece((planes - 1,)),
+            VMEM((3, 2, planes, 3 * deep, PAIR), bf16),
+            VMEM((planes, 3 * deep, PAIR), bf16),
+            VMEM((planes - 1, 3 * deep, PAIR), bf16),
+            VMEM((pairs, 8, PAIR), f32),
+            VMEM((4, 8, PAIR), f32),
+            VMEM((8, PAIR), f32),
+            VMEM((planes, 8, PAIR), f32),
+            VMEM((2, rows_dec, width), bf16),
+            VMEM((2, rows_dec, width), bf16),
+            VMEM((rows_dec // BLOCK, BLOCK, width), bf16),
+            VMEM((rows_dec // BLOCK, BLOCK, width), bf16),
+            VMEM((2, rows_dec, width), f32),
+            VMEM((2 * rows_src, width), bf16),
+            VMEM((2 * rows_src, width), bf16),
+            VMEM((rows_src, width), bf16),
+            VMEM((2, rows_src, width), f32),
+        ]
+        small = ((deep, PAIR), f32)
+        outs = call(
+            partial(last_kernel, True, planes),
+            [
+                (decoder_in.shape, bf16),
+                (decoder_in.shape, f32),
+                (source_states.shape, f32),
+                *[small] * 8,
+                (ffn_expand.shape, f32),
+                (ffn_reduce.shape, f32),
+                ((8, PAIR), f32),
+            ],
+            *operands,
+            part_a,
+            part_b,
+            part_c,
+            grad_source,
+            out_rows,
+            scratch=work,
+            smem=2,
+            spaces=everywhere,
+            out_spaces={at: pl.ANY for at in range(3)},
+            params=pltpu.CompilerParams(
+                vmem_limit_bytes=VMEM_LIMIT, collective_id=1, has_side_effects=True
+            ),
+        )
+        (decoder_out, grad_decoder, grad_src, dwq, dwk, dwv, *rest, dw1, dw2, dgains) = outs
+        dwo, dwcq, dwck, dwcv, dwco = rest
+    else:
+        own_grad, other_grad, part_qkv, dgains = call(
+            partial(last_kernel, False, planes),
+            [((own, width), f32), ((own, width), bf16), part_q, ((8, width), f32)],
+            *operands,
+            scratch=work,
+            smem=2,
+            spaces=everywhere,
+        )
+        crossing = jnp.concatenate([other_grad, grad_source[2 * rows_src :]], axis=0)
+        returned = swapped(crossing, "seq", 1).astype(f32)
+        grad_rows = own_grad + returned[:own]
+        source_rows = grad_source[: 2 * rows_src].astype(f32) + returned[own:]
+        homeward = [grad_rows[rows_dec:].astype(bf16), source_rows[rows_src:].astype(bf16)]
+        came = swapped(jnp.concatenate([out_rows[rows_dec:], *homeward], axis=0), "seq", 2)
+
+        def both_sentences(mine, theirs):
+            theirs = theirs.astype(mine.dtype)
+            return jnp.where(chip == 0, jnp.stack([mine, theirs]), jnp.stack([theirs, mine]))
+
+        decoder_out = both_sentences(out_rows[:rows_dec], came[:rows_dec])
+        grad_decoder = both_sentences(grad_rows[:rows_dec], came[rows_dec : 2 * rows_dec])
+        grad_src = both_sentences(source_rows[:rows_src], came[2 * rows_dec :])
+
+        def summed(blocks, start, count, chunks=1):
+            grad = from_blocks(blocks[:, :, :, start : start + chunks * count], chunks)
+            grad = lax.psum_scatter(grad.astype(f32), "dp", scatter_dimension=0, tiled=True)
+            return lax.psum_scatter(grad, "seq", scatter_dimension=1, tiled=True)
+
+        step = width // 8
+        dwq, dwk, dwv = [summed(part_qkv, at * step, step) for at in range(3)]
+        dwo, dwcq, dwck, dwcv, dwco = [summed(part_a, at * step, step) for at in range(5)]
+        dw1 = summed(part_b, 0, step, hidden_width // width)
+        tall = part_c.reshape(seq_size, 2, 4, hidden_width // 8 // PAIR, PAIR, PAIR)
+        dw2 = summed(tall.swapaxes(4, 5).reshape(part_c.shape), 0, hidden_width // 8)
+        dgains = lax.psum(dgains, "dp")
+        dgains = lax.psum_scatter(dgains, "seq", scatter_dimension=1, tiled=True)
+    return (
+        decoder_out,
+        grad_decoder,
+        grad_src,
+        dwq,
+        dwk,
+        dwv,
+        dwo,
+        dwcq,
+        dwck,
+        dwcv,
+        dwco,
+        dw1,
+        dw2,
+        dgains[:3],
     )
-    own_grad, other_grad, dwq, dwk, dwv, dgain_one = call(
-        partial(close_kernel, own),
-        [
-            ((own, width), f32),
-            ((total - own, width), bf16),
-            square,
-            square,
-            square,
-            ((8, width), f32),
-        ],
-        x_all,
-        qkv,
-        gains,
-        dqt,
-        dk,
-        dv,
-        grad_self,
-        scratch=[VMEM((width, width), bf16)] * 3,
-    )
-
-    half_src = all_src // 2
-    crossing = jnp.concatenate([other_grad, grad_source[half_src:].astype(bf16)], axis=0)
-    returned = swapped(crossing, "seq", 1).astype(f32)
-    grad_rows = own_grad + returned[:own]
-    source_rows = grad_source[:half_src] + returned[own:]
-    homeward = jnp.concatenate(
-        [out_rows[rows_dec:], grad_rows[rows_dec:].astype(bf16), source_rows[rows_src:].astype(bf16)],
-        axis=0,
-    )
-    came = swapped(homeward, "seq", 2)
-
-    def both_sentences(mine, theirs):
-        return jnp.where(chip == 0, jnp.stack([mine, theirs]), jnp.stack([theirs, mine]))
-
-    decoder_out = both_sentences(out_rows[:rows_dec], came[:rows_dec])
-    grad_decoder = both_sentences(grad_rows[:rows_dec], came[rows_dec : 2 * rows_dec].astype(f32))
-    grad_src = both_sentences(source_rows[:rows_src], came[2 * rows_dec :].astype(f32))
-
-    def shares(grad, depth, columns):
-        parts = grad.reshape(dp_size, depth, seq_size, columns).swapaxes(1, 2)
-        return parts.reshape(dp_size, seq_size, depth * columns // PAIR, PAIR)
-
-    dgains = jnp.stack([dgain_one[0], dgain[1], dgain[2]])
-    dgains = jnp.concatenate([dgains, jnp.zeros((13, width), f32)], axis=0)
-    dgains = dgains.reshape(1, 16, seq_size, PAIR).swapaxes(1, 2)
-    dgains = jnp.broadcast_to(dgains, (dp_size, seq_size, 16, PAIR))
-    dw2_parts = dw2t.reshape(seq_size, PAIR, dp_size, deep_two).transpose(2, 0, 1, 3)
-    dw2_parts = dw2_parts.reshape(dp_size, seq_size, deep_two, PAIR)
-    grads = [shares(grad, deep, PAIR) for grad in (dwq, dwk, dwv, dwo, dwcq, dwck, dwcv, dwco)]
-    grads += [shares(dw1, deep, wide * PAIR), dw2_parts, dgains]
-    grads = jnp.concatenate([grad.astype(bf16) for grad in grads], axis=2)
-    total = lax.psum_scatter(
-        grads.reshape(devices, -1, PAIR), both, scatter_dimension=0, tiled=True
-    )[0].astype(f32)
-    outs = [total[at * deep : (at + 1) * deep] for at in range(8)]
-    start = 8 * deep
-    outs.append(total[start : start + wide * deep].reshape(deep, wide * PAIR))
-    start += wide * deep
-    outs.append(total[start : start + deep_two].reshape(PAIR, deep_two).T)
-    start += deep_two
-    outs.append(total[start : start + 3])
-    return (decoder_out, grad_decoder, grad_src, *outs)
 
 
 def solution(mesh):

time: 461 us -> 268 us (0.58)
  waiting for transfers between devices: 144 us -> 0 us
  local copies, waits for them, and re-layouts: 43.5 us -> 12.1 us
  other arithmetic: 22.1 us -> 1.28 us
  Pallas kernels: 234 us -> 254 us
  between operations: 14.3 us -> 0.76 us
    reduce_scatter x1 -> x0, waiting for transfers between devices: 88.2 us -> none  [body(): lax.psum_scatter(grads.reshape(devices, -1, PAIR), both, scatter_dimensio...]
    ppermute x2 -> x0, waiting for transfers between devices: 56 us -> none  [swapped(): return lax.ppermute(value, axis, pairs)]
    convert_element_type x15 -> x0, local copies, waits for them, and re-layouts: 21.3 us -> none  [body(): grads = jnp.concatenate([grad.astype(bf16) for grad in grads], axis=2)]
    pallas_call x4 -> x3, Pallas kernels: 234 us -> 254 us  [call(): pl.pallas_call(kernel, out_shape=[jax.ShapeDtypeStruct(shape, kind) for s...]
    convert_element_type x12 -> x0, other arithmetic: 13.2 us -> none  [the longest x10 11.8 us: body(): grads = jnp.concatenate([grad.astype(bf16) for grad in grads], axis=2)]
    unnamed x35 -> x37, local copies, waits for them, and re-layouts: 16 us -> 10.7 us
  transfers between devices with their start and end apart: 3 -> 0, of which waited for: 3 -> 0; matrix products, arithmetic and copies ran while one was open for 2% -> 0% of each run, Pallas kernels for 0% -> 0%
where the time goes in v2:
time: 268 us
  Pallas kernels  254 us (95%)
  local copies, waits for them, and re-layouts  12.1 us (5%)
    pallas_call x3, Pallas kernels, call(): pl.pallas_call(kernel, out_shape=[jax.ShapeDtypeStruct(shape, kind) for s...  254 us
    unnamed x37, local copies, waits for them, and re-layouts  10.7 us

profile of v2, /device:TPU:0, one launch (start us, length us, event | category | flops | bytes accessed | tf_op | source)
XLA Modules:
  0.0 267.9 jit_solution(9885733272312536713)
XLA Ops:
  0.6 1.3 pad_convert_fusion.refs_13_
  1.9 87.6 %shard_map.272 = (bf16[2048,512]{1,0:T(8,128)(2,1)}, bf16[512,512]{1,0:T(8,128)(2,1)}, bf16[1024,512]{1,0:T(8,128)(2,1)}, bf16[4,2,4,192,128]{4,3,2,1,0:T(8,128)...) custom-call(s32[16]{0:T(128)} %source_len_ref.5, ...), custom_call_target="tpu_custom_call" | custom-call | tf_op jit(solution)/shard_map/pallas_call | solution.py:1264
  89.5 68.9 %shard_map.273 = (bf16[1024,512]{1,0:T(8,128)(2,1)}, bf16[4,1024,128]{2,1,0:T(8,128)(2,1)}, f32[1024,512]{1,0:T(8,128)}, bf16[4,2,4,320,128]{4,3,2,1,0:T(8,128)(...) custom-call(s32[16]{0:T(128)} %source_len_ref.5, ...), custom_call_target="tpu_custom_call" | custom-call | tf_op jit(solution)/shard_map/pallas_call | solution.py:1264
  158.3 97.4 %shard_map.274 = (bf16[2,512,512]{2,1,0:T(8,128)(2,1)}, f32[2,512,512]{2,1,0:T(8,128)}, f32[2,128,512]{2,1,0:T(8,128)}, f32[64,128]{1,0:T(8,128)}, f32[64,128]{1...) custom-call(s32[16]{0:T(128)} %source_len_ref.5, ...), custom_call_target="tpu_custom_call" | custom-call | tf_op jit(solution)/shard_map/pallas_call | solution.py:1264
  255.7 0.0 copy-start
  255.7 1.4 slice.3
  257.1 2.3 copy.44
  259.4 0.0 copy-done
  259.4 0.0 copy-start.9
  259.4 0.0 copy-start.8
  259.5 1.3 copy.45
  260.8 0.8 copy.46
  261.6 0.6 copy.47
  262.2 0.0 copy-done.10
  262.2 0.6 copy.48
  262.9 0.6 copy.49
  263.5 0.6 copy.50
  264.1 0.6 copy.51
  264.7 0.0 copy-done.6
  264.7 0.6 copy.52
  265.3 0.6 copy.53
  265.9 0.6 copy.54
  266.6 0.7 copy.55
  267.2 0.7 copy.56
  (18 shorter events, 0.0 us)
Async XLA Ops:
  255.7 3.7 %copy-start = (f32[2,512,512]{2,1,0:T(8,128)S(1)}, f32[2,512,512]{2,1,0:T(8,128)}, u32[]{:S(2)}) copy-start(f32[2,512,512]{2,1,0:T(8,128)} %get-tuple-element.99) | copy-start | bytes 6291460
  259.4 1.4 copy-start.1
  259.4 2.2 copy-start.11
  259.4 2.8 %copy-start.10 = (f32[64,128]{1,0:T(8,128)S(1)}, f32[64,128]{1,0:T(8,128)}, u32[]{:S(2)}) copy-start(f32[64,128]{1,0:T(8,128)} %get-tuple-element.102) | copy-start | bytes 98308
  259.4 3.4 %copy-start.9 = (f32[64,128]{1,0:T(8,128)S(1)}, f32[64,128]{1,0:T(8,128)}, u32[]{:S(2)}) copy-start(f32[64,128]{1,0:T(8,128)} %get-tuple-element.103) | copy-start | bytes 98308
  259.4 4.0 %copy-start.8 = (f32[64,128]{1,0:T(8,128)S(1)}, f32[64,128]{1,0:T(8,128)}, u32[]{:S(2)}) copy-start(f32[64,128]{1,0:T(8,128)} %get-tuple-element.104) | copy-start | bytes 98308
  259.4 4.7 %copy-start.7 = (f32[64,128]{1,0:T(8,128)S(1)}, f32[64,128]{1,0:T(8,128)}, u32[]{:S(2)}) copy-start(f32[64,128]{1,0:T(8,128)} %get-tuple-element.105) | copy-start | bytes 98308
  259.5 5.3 %copy-start.6 = (f32[64,128]{1,0:T(8,128)S(1)}, f32[64,128]{1,0:T(8,128)}, u32[]{:S(2)}) copy-start(f32[64,128]{1,0:T(8,128)} %get-tuple-element.106) | copy-start | bytes 98308
  259.5 5.9 %copy-start.5 = (f32[64,128]{1,0:T(8,128)S(1)}, f32[64,128]{1,0:T(8,128)}, u32[]{:S(2)}) copy-start(f32[64,128]{1,0:T(8,128)} %get-tuple-element.107) | copy-start | bytes 98308
  259.5 6.5 %copy-start.4 = (f32[64,128]{1,0:T(8,128)S(1)}, f32[64,128]{1,0:T(8,128)}, u32[]{:S(2)}) copy-start(f32[64,128]{1,0:T(8,128)} %get-tuple-element.108) | copy-start | bytes 98308
  259.5 7.1 %copy-start.3 = (f32[64,512]{1,0:T(8,128)S(1)}, f32[64,512]{1,0:T(8,128)}, u32[]{:S(2)}) copy-start(f32[64,512]{1,0:T(8,128)} %get-tuple-element.109) | copy-start | bytes 393220
  259.5 7.7 %copy-start.2 = (f32[256,128]{1,0:T(8,128)S(1)}, f32[256,128]{1,0:T(8,128)}, u32[]{:S(2)}) copy-start(f32[256,128]{1,0:T(8,128)} %get-tuple-element.110) | copy-start | bytes 393220

commit v3 on v2

--- a/solution.py
+++ b/solution.py
@@ -127,13 +127,18 @@
     )
 
 
-def entry_barrier(partners):
-    barrier = pltpu.get_barrier_semaphore()
+def greet(partners):
     for partner in partners:
         pl.semaphore_signal(
-            barrier, inc=1, device_id=partner, device_id_type=pl.DeviceIdType.MESH
+            pltpu.get_barrier_semaphore(),
+            inc=1,
+            device_id=partner,
+            device_id_type=pl.DeviceIdType.MESH,
         )
-    pl.semaphore_wait(barrier, len(partners))
+
+
+def await_greetings(partners):
+    pl.semaphore_wait(pltpu.get_barrier_semaphore(), len(partners))
 
 
 class Where:
@@ -217,6 +222,7 @@
             q_out, k_out, v_out, mixed_out, extra_out,
             x_ref, qkv_ref, gain_ref, hidden_ref, weight_ref, mask_ref,
             q_ref, k_ref, v_ref, mixed_ref, extra_ref, send, receive,
+            stage_a, stage_b, stage_c, stage_s, gain_block,
         ) = refs
     else:
         (
@@ -239,15 +245,13 @@
         x_slots = [x_ref.at[slot * rows : (slot + 1) * rows] for slot in range(4)]
         few = source_ref.shape[1]
         s_slots = [source_out.at[slot * few : (slot + 1) * few] for slot in range(4)]
-        c_slots = [cotangent_out.at[slot * rows : (slot + 1) * rows] for slot in range(2)]
         local_x = semaphores.local(decoder_ref.at[chip], x_slots[0])
-        local_gain = semaphores.local(gain_in, gain_ref.at[place])
         mine = qkv_ref.at[place, side, plane]
         local_qkv = [
             semaphores.local(ref, mine.at[at * deep : (at + 1) * deep])
             for at, ref in enumerate((wq_in, wk_in, wv_in))
         ]
-        first = [local_x, local_gain, *local_qkv]
+        first = [local_x, *local_qkv]
         wo_in, wcq_in, wck_in, wcv_in, wco_in, w1_in, w2_in = later_in
         mine_a = later_a.at[place, side, plane]
         mine_b = later_b.at[place, side, plane]
@@ -255,24 +259,31 @@
         wide = w1_in.shape[1] // PAIR
         local_later = [
             [
-                semaphores.local(ref, mine_a.at[at * deep : (at + 1) * deep])
+                semaphores.local(ref, stage_a.at[at * deep : (at + 1) * deep])
                 for at, ref in enumerate((wo_in, wcq_in, wck_in, wcv_in, wco_in))
             ],
             [
                 semaphores.local(
-                    w1_in.at[:, at * PAIR : (at + 1) * PAIR], mine_b.at[at * deep : (at + 1) * deep]
+                    w1_in.at[:, at * PAIR : (at + 1) * PAIR], stage_b.at[at * deep : (at + 1) * deep]
                 )
                 for at in range(wide)
             ],
-            [semaphores.local(w2_in, mine_c)],
+            [semaphores.local(w2_in, stage_c)],
         ]
-        local_rest = [
-            semaphores.local(source_ref.at[chip], s_slots[0]),
-            semaphores.local(cotangent_ref.at[chip], c_slots[0]),
+        stores = [
+            semaphores.local(stage_a, mine_a),
+            semaphores.local(stage_b, mine_b),
+            semaphores.local(stage_c, mine_c),
         ]
-        for copy in first + local_later[0] + local_later[1] + local_later[2] + local_rest:
+        source_load = semaphores.local(source_ref.at[chip], stage_s)
+        source_store = semaphores.local(stage_s, s_slots[0])
+        greet(where.everyone())
+        gain_block[...] = jnp.zeros(gain_block.shape, f32)
+        gain_block[0 : gain_in.shape[0], :] = gain_in[...].astype(f32)
+        gain_ref[place] = gain_block[...]
+        for copy in first + local_later[0] + local_later[1] + local_later[2] + [source_load]:
             copy.start()
-        entry_barrier(where.everyone())
+        await_greetings(where.everyone())
 
         x_cross = semaphores.remote(decoder_ref.at[1 - chip], x_slots[1], where.other_chip)
         x_core = semaphores.remote(decoder_ref.at[chip], x_slots[2], where.other_core)
@@ -280,9 +291,9 @@
         s_cross = semaphores.remote(source_ref.at[1 - chip], s_slots[1], where.other_chip)
         s_core = semaphores.remote(source_ref.at[chip], s_slots[2], where.other_core)
         s_pass = semaphores.remote(s_slots[1], s_slots[3], where.other_core)
-        c_cross = semaphores.remote(cotangent_ref.at[1 - chip], c_slots[1], where.other_chip)
+        c_cross = semaphores.remote(cotangent_ref.at[1 - chip], cotangent_out, where.other_chip)
         gain_sends = [
-            semaphores.remote(gain_in, gain_ref.at[place], partner)
+            semaphores.remote(gain_block, gain_ref.at[place], partner)
             for partner in (where.other_core, where.other_chip, where.diagonal)
         ]
         qkv_planes = [semaphores.remote(mine, mine, partner) for partner in where.other_planes]
@@ -294,22 +305,34 @@
         across = column(2)
         qkv_pass = semaphores.remote(qkv_ref.at[across], qkv_ref.at[across], where.other_core)
         later = []
-        for buffer in (later_a, later_b, later_c):
+        for buffer, stage in ((later_a, stage_a), (later_b, stage_b), (later_c, stage_c)):
             block = buffer.at[place, side, plane]
+            mine_side, across_side = buffer.at[place, side], buffer.at[across, side]
+            if buffer is later_c:
+                first = [semaphores.remote(stage, block, where.other_chip)]
+                far = buffer.at[across, side, plane]
+                second = [
+                    semaphores.remote(stage, block, where.other_side),
+                    semaphores.remote(far, far, where.other_side),
+                ]
+                others = [buffer.at[at, 1 - side, plane] for at in (place, across)]
+                kept = [(stage, block), (far, far)] + [(one, one) for one in others]
+            else:
+                first = [semaphores.remote(mine_side, mine_side, where.other_chip)]
+                second = [
+                    semaphores.remote(one, one, where.other_side)
+                    for one in (mine_side, across_side)
+                ]
+                kept = [(stage, block)]
             later.append(
                 dict(
-                    planes=[semaphores.remote(block, block, p) for p in where.other_planes],
-                    chip=[
-                        semaphores.remote(
-                            buffer.at[place, side], buffer.at[place, side], where.other_chip
-                        )
+                    planes=[
+                        semaphores.remote(one, other, partner)
+                        for one, other in kept
+                        for partner in where.other_planes
                     ],
-                    side=[
-                        semaphores.remote(
-                            buffer.at[at, side], buffer.at[at, side], where.other_side
-                        )
-                        for at in (place, across)
-                    ],
+                    first=first,
+                    second=second,
                     core=[
                         semaphores.remote(buffer.at[at], buffer.at[at], where.other_core)
                         for at in (place, across)
@@ -325,17 +348,22 @@
             for copy in copies:
                 copy.wait_recv()
 
+        begin(gain_sends)
+        for copy in local_qkv:
+            copy.wait()
+        begin(qkv_planes)
         x_cross.start()
         x_core.start()
-        for copy in [local_gain, *local_qkv]:
-            copy.wait()
-        begin(gain_sends)
-        begin(qkv_planes)
-        begin([s_cross, s_core])
-        for copies, piece in zip(local_later, later):
+        begin([s_core])
+        for copies in local_later:
             for copy in copies:
                 copy.wait()
-            begin(piece["planes"])
+        source_load.wait()
+        begin([*stores, source_store])
+        a, b, c = later
+        begin(c["first"])
+        begin(a["planes"])
+        begin(b["planes"])
 
     length = source_len_ref[where.group * 2 + chip] * upsample_ref[where.group * 2 + chip]
     mask_columns(chip, core, rows, total, BLOCK, length, mask_ref)
@@ -384,14 +412,21 @@
         hide(2)
         arrive(qkv_planes)
         qkv_side.start()
-        arrive([x_cross])
-        x_pass.start()
-        hide(1)
         arrive([qkv_side])
-        begin([qkv_core, qkv_chip])
+        begin([qkv_core])
         take_weights(place)
         project(place, 0, 1)
         project(place, 2, 1)
+        arrive([x_cross])
+        x_pass.start()
+        arrive(a["planes"])
+        for copy in [*stores, source_store]:
+            copy.wait()
+        begin(a["first"])
+        arrive(c["first"])
+        begin(c["second"])
+        begin([qkv_chip])
+        hide(1)
         project(place, 1, 1)
         arrive([x_pass])
         hide(3)
@@ -430,49 +465,42 @@
         turn = index // blocks
         pair = column(turn)
         if comm:
-            a, b, c = later
-
-            @pl.when(index == 0)
-            def _():
-                arrive(a["planes"])
-                begin(a["chip"])
-
             @pl.when(index == 1)
             def _():
+                arrive(c["second"])
+                begin(c["planes"])
                 arrive(b["planes"])
-                begin(b["chip"])
-                arrive(c["planes"])
-                begin(c["chip"])
+                begin(b["first"])
+                begin([s_cross, c_cross])
 
             @pl.when(index == 2)
             def _():
                 arrive([qkv_core])
-                arrive(a["chip"])
-                begin(a["side"])
-
-            @pl.when(index == 3)
+                arrive(a["first"])
+                begin(a["second"])
+
+            @pl.when(index == 4)
             def _():
                 arrive([qkv_chip])
                 qkv_pass.start()
-                arrive(b["chip"])
-                begin(b["side"])
-                local_rest[0].wait()
-                arrive([s_cross])
-                s_pass.start()
-                c_cross.start()
-
-            @pl.when(index == 4)
+
+            @pl.when(index == 5)
             def _():
-                arrive(c["chip"])
-                begin(c["side"])
-                arrive(a["side"])
+                arrive(b["first"])
+                begin(b["second"])
+                arrive(a["second"])
                 begin(a["core"])
 
             @pl.when(index == 6)
             def _():
                 arrive([qkv_pass])
-                arrive(b["side"])
-                begin(b["core"])
+                arrive([s_cross])
+                s_pass.start()
+
+            @pl.when(index == 7)
+            def _():
+                arrive(c["planes"])
+                begin(c["core"])
 
         @pl.when((index % blocks == 0) & (index > 0))
         def _():
@@ -501,10 +529,8 @@
         gain_local = pltpu.make_async_copy(gain_ref, gain_out, send.at[first_out + 22])
         for copy in (x_local, qkv_local, gain_local):
             copy.start()
-        c = later[2]
-        arrive(c["side"])
-        begin(c["core"])
-        local_rest[1].wait()
+        arrive(b["second"])
+        begin(b["core"])
         arrive([s_core, s_pass, c_cross])
         for piece in later:
             arrive(piece["core"])
@@ -550,7 +576,8 @@
     send_ref,
     x_any,
     mixed_ref,
-    cotangent_ref,
+    cotangent_any,
+    cotangent_far,
     source_ref,
     later_a,
     later_b,
@@ -586,6 +613,7 @@
     dck_ref,
     dcv_ref,
     x_sem,
+    cotangent_ref,
     cm_s,
     extra_s,
     dqt_s,
@@ -597,10 +625,21 @@
     pairs = mixed_ref.shape[0]
     hidden_width = w1_ref.shape[1]
     chunk = 512
-    x_copy = pltpu.make_async_copy(x_any.at[:rows_own], x_ref, x_sem)
-    x_copy.start()
     where = Where(planes)
     chip, core = where.chip, where.core
+    half = rows_own // 2
+    loads = [
+        pltpu.make_async_copy(source, target, x_sem.at[at])
+        for at, (source, target) in enumerate(
+            (
+                (x_any.at[:rows_own], x_ref),
+                (cotangent_any.at[chip], cotangent_ref.at[:half]),
+                (cotangent_far, cotangent_ref.at[half:]),
+            )
+        )
+    ]
+    for copy in loads:
+        copy.start()
     few = source_ref.shape[0]
     deep = width // 8
     for at, ref in enumerate((wo_ref, wcq_ref, wck_ref, wcv_ref, wco_ref)):
@@ -648,7 +687,8 @@
         return 0
 
     lax.fori_loop(0, few // BLOCK, source_step, 0)
-    x_copy.wait()
+    for copy in loads:
+        copy.wait()
 
     def step(index, _):
         rows = block_at(index, BLOCK)
@@ -788,8 +828,9 @@
     refs = refs[11:]
     if comm:
         (part_a, part_b, part_c, source_any, rows_any) = refs[:5]
-        (decoder_out, grad_out, source_out, *weight_outs, gain_out) = refs[5:19]
-        refs = refs[19:]
+        (rows_land, grad_out, cross_land, source_out, source_far) = refs[5:10]
+        (*weight_outs, gain_out) = refs[10:21]
+        refs = refs[21:]
     else:
         (own_out, other_out, part_out, gain_out) = refs[:4]
         refs = refs[4:]
@@ -861,16 +902,17 @@
             keep_a, keep_b, keep_c, core_a, core_b, core_c, far_a, far_b, far_c,
             near_a, near_b, near_c, planes_a, planes_b, planes_c,
             land_q, far_q, planes_q, gain_send, gain_land, gain_far, gain_planes, grads_send,
-            grads_land, cross_send, cross_land, stage, source_s, source_land, source_far, stage_s,
+            grads_land, cross_send, stage, source_s, source_land, stage_s,
         ) = refs
         place, across = where.place, where.column(2)
         pieces = []
-        for part, keep, land, far, near, land_planes, side_first in (
-            (part_a, keep_a, core_a, far_a, near_a, planes_a, True),
-            (part_b, keep_b, core_b, far_b, near_b, planes_b, False),
-            (part_c, keep_c, core_c, far_c, near_c, planes_c, True),
+        for part, keep, land, far_land, near_land, land_planes, order in (
+            (part_a, keep_a, core_a, far_a, near_a, planes_a, "yxz"),
+            (part_b, keep_b, core_b, far_b, near_b, planes_b, "yzx"),
+            (part_c, keep_c, core_c, far_c, near_c, planes_c, "xyz"),
         ):
-            piece = dict(keep=keep, land=land, far=far, near=near, planes=land_planes)
+            piece = dict(keep=keep, land=land, order=order)
+            piece.update(far_land=far_land, near_land=near_land, planes=land_planes)
             piece["load"] = [
                 semaphores.local(part.at[place], keep.at[0]),
                 semaphores.local(part.at[across], keep.at[1]),
@@ -879,32 +921,38 @@
                 semaphores.remote(part.at[where.column(1)], land.at[0], where.other_core),
                 semaphores.remote(part.at[where.column(3)], land.at[1], where.other_core),
             ]
-            if side_first:
+            if order[0] == "y":
                 piece["far"] = [
-                    semaphores.remote(keep.at[at, 1 - side], far.at[at], where.other_side)
+                    semaphores.remote(keep.at[at, 1 - side], far_land.at[at], where.other_side)
                     for at in (0, 1)
                 ]
-                piece["near"] = [semaphores.remote(keep.at[1, side], near, where.other_chip)]
             else:
                 piece["far"] = [
-                    semaphores.remote(keep.at[1, at], far.at[at], where.other_chip)
+                    semaphores.remote(keep.at[1, at], far_land.at[at], where.other_chip)
                     for at in (0, 1)
                 ]
-                piece["near"] = [semaphores.remote(keep.at[0, 1 - side], near, where.other_side)]
+            if order == "yzx":
+                near = (keep.at[1, side, plane], near_land.at[0], where.other_chip)
+            elif order == "yxz":
+                near = (keep.at[1, side], near_land, where.other_chip)
+            else:
+                near = (keep.at[0, 1 - side], near_land, where.other_side)
+            piece["near"] = [semaphores.remote(*near)]
             piece["last"] = [
                 semaphores.remote(
-                    keep.at[0, side, (plane + step) % planes],
-                    land_planes.at[step - 1],
+                    keep.at[at, side, (plane + step) % planes],
+                    land_planes.at[at, step - 1],
                     where.other_planes[step - 1],
                 )
+                for at in ((0, 1) if order == "yzx" else (0,))
                 for step in range(1, planes)
             ]
-            piece["side_first"] = side_first
             pieces.append(piece)
         a, b, c = pieces
         owners = (where.diagonal, where.other_chip, where.other_core)
+        hops = (where.other_core, where.other_chip, where.other_core)
         send_q = [
-            semaphores.remote(part_s.at[turn], land_q.at[turn], owners[turn]) for turn in range(3)
+            semaphores.remote(part_s.at[turn], land_q.at[turn], hops[turn]) for turn in range(3)
         ]
         side_q = semaphores.remote(part_s.at[3, 1 - side], far_q, where.other_side)
         plane_q = [
@@ -926,8 +974,7 @@
             )
             for step in range(1, planes)
         ]
-        rows_local = semaphores.local(rows_any.at[:rows], decoder_out.at[chip])
-        rows_cross = semaphores.remote(rows_any.at[rows:], decoder_out.at[chip], where.other_chip)
+        rows_cross = semaphores.remote(rows_any.at[rows:], rows_land, where.other_chip)
         few = source_any.shape[0] // 4
         source_local = semaphores.local(source_any.at[: 2 * few], source_s)
         source_core = semaphores.remote(source_any.at[2 * few :], source_land, where.other_core)
@@ -940,21 +987,12 @@
             semaphores.remote(cross_send.at[at], cross_land.at[at], where.other_chip)
             for at in range(rows // BLOCK)
         ]
-        stage_out = [
-            semaphores.local(stage.at[at], grad_out.at[chip if at == 0 else 1 - chip])
-            for at in range(2)
-        ]
-        source_outs = [
-            semaphores.local(stage_s.at[at], source_out.at[chip if at == 0 else 1 - chip])
-            for at in range(2)
-        ]
+        stage_out = semaphores.local(stage, grad_out)
+        source_own = semaphores.local(stage_s, source_out)
         for piece in pieces:
             begin(piece["load"])
-        begin([rows_local, source_local])
-        entry_barrier(where.everyone())
-        for piece in pieces:
-            begin(piece["core"])
-        begin([source_core, rows_cross])
+        begin([source_local])
+        greet(where.everyone())
 
         def add_in(ref, land):
             def add(at, _):
@@ -975,26 +1013,35 @@
         def add_far(piece):
             arrive(piece["far"])
             for at in (0, 1):
-                if piece["side_first"]:
+                if piece["order"][0] == "y":
                     add_in(piece["keep"].at[at, side], piece["far_land"].at[at])
                 else:
                     add_in(piece["keep"].at[0, at], piece["far_land"].at[at])
-            begin(piece["near"])
+            begin(piece["last" if piece["order"] == "yzx" else "near"])
 
         def add_near(piece):
             arrive(piece["near"])
             add_in(piece["keep"].at[0, side], piece["near_land"])
             begin(piece["last"])
 
+        def over_planes(piece, at):
+            value = piece["keep"][at, side, plane].astype(f32)
+            for step in range(planes - 1):
+                value = value + piece["planes"][at, step].astype(f32)
+            return value
+
+        def add_planes(piece):
+            arrive(piece["last"])
+            for at in (0, 1):
+                piece["keep"][at, side, plane] = over_planes(piece, at).astype(bf16)
+            begin(piece["near"])
+
         def finish(piece):
+            if piece["order"] == "yzx":
+                arrive(piece["near"])
+                return piece["keep"][0, side, plane].astype(f32) + piece["near_land"][0].astype(f32)
             arrive(piece["last"])
-            value = piece["keep"][0, side, plane].astype(f32)
-            for step in range(planes - 1):
-                value = value + piece["planes"][step].astype(f32)
-            return value
-
-        for piece, far, near in ((a, far_a, near_a), (b, far_b, near_b), (c, far_c, near_c)):
-            piece["far_land"], piece["near_land"] = far, near
+            return over_planes(piece, 0)
 
     mask_columns(chip, core, rows, total, BLOCK, length, values_s.at[:, PAIR:])
     keys_s[:, PAIR:] = values_s[:, PAIR:]
@@ -1009,6 +1056,11 @@
         return 0
 
     lax.fori_loop(0, total // BLOCK, hide, 0)
+    if comm:
+        await_greetings(where.everyone())
+        for piece in pieces:
+            begin(piece["core"])
+        begin([source_core, rows_cross])
 
     def take_weights(turn, pair):
         for part in range(3):
@@ -1035,6 +1087,7 @@
             @pl.when(index == 1)
             def _():
                 add_core(a)
+                add_core(c)
                 add_core(b)
                 source_local.wait()
                 arrive([source_core])
@@ -1043,30 +1096,33 @@
                     value = source_s[r, :].astype(f32) + source_land[r, :].astype(f32)
                     source_s[r, :] = value.astype(bf16)
                     if half == 0:
-                        stage_s[0] = value
-                begin([source_cross, source_outs[0]])
+                        stage_s[...] = value
+                begin([source_cross, source_own])
 
             @pl.when(index == 3)
             def _():
                 add_far(a)
-                add_core(c)
+                add_far(c)
 
             @pl.when(index == 4)
             def _():
-                add_far(b)
+                arrive([send_q[0]])
+                for half in range(2):
+                    add_in(part_s.at[1, half], land_q.at[0, half])
+                send_q[1].start()
 
             @pl.when(index == 5)
             def _():
+                add_far(b)
                 add_near(a)
-                add_far(c)
 
             @pl.when(index == 6)
             def _():
-                add_near(b)
+                add_near(c)
 
             @pl.when(index == 7)
             def _():
-                add_near(c)
+                add_planes(b)
 
         @pl.when(index % blocks == 0)
         def _():
@@ -1123,7 +1179,7 @@
                     part_s[turn, at % 2, at // 2, part * deep : (part + 1) * deep, :] = value
 
         if comm:
-            for sent in range(3):
+            for sent in (0, 2):
 
                 @pl.when(index == sent * blocks + blocks - 1)
                 def _():
@@ -1181,7 +1237,7 @@
     def add_q(at, _):
         for half in range(2):
             value = part_s[3, half, at].astype(f32)
-            for turn in range(3):
+            for turn in (1, 2):
                 value = value + land_q[turn, half, at].astype(f32)
             part_s[3, half, at] = value.astype(bf16)
         return 0
@@ -1196,33 +1252,36 @@
         grads_core[slot - 2].start()
 
     other_rows(3)
-    arrive(send_q)
+    arrive(send_q[1:])
     lax.fori_loop(0, planes, add_q, 0)
     side_q.start()
     other_rows(2)
+
+    def own_rows(row, _):
+        r, back = row_back(row, True)
+        total_s[r, :] = back + grad_self_s[r, :]
+        return 0
+
+    lax.fori_loop(0, 2 * per, own_rows, 0)
+    for at in range(pairs):
+        gain_send[at] = dgain_s[:, at * PAIR : (at + 1) * PAIR]
+    begin(gain_group)
     arrive([grads_core[1]])
     for row in range(per):
-        r, back = row_back(per + row, True)
-        value = back + grad_self_s[r, :] + grads_land[1, row * BLOCK : (row + 1) * BLOCK, :].astype(f32)
-        cross_send[row] = value.astype(bf16)
+        r = slice(row * BLOCK, (row + 1) * BLOCK)
+        value = total_s[rows + row * BLOCK : rows + (row + 1) * BLOCK, :]
+        cross_send[row] = (value + grads_land[1, r, :].astype(f32)).astype(bf16)
         grads_cross[row].start()
     arrive([side_q])
     add_in(part_s.at[3, side], far_q)
     begin(plane_q)
-    arrive([grads_core[0]])
-    for row in range(per):
-        r, back = row_back(row, True)
-        r_own = slice(row * BLOCK, (row + 1) * BLOCK)
-        stage[0, r_own, :] = back + grad_self_s[r, :] + grads_land[0, r_own, :].astype(f32)
-    stage_out[0].start()
-
-    for at in range(pairs):
-        gain_send[at] = dgain_s[:, at * PAIR : (at + 1) * PAIR]
-    begin(gain_group)
-    sums = [finish(piece) for piece in pieces]
     arrive(gain_group)
     gain_land[3] = gain_send[place] + gain_land[0] + gain_land[1] + gain_land[2]
     gain_side.start()
+    arrive([grads_core[0]])
+    stage[...] = total_s[:rows, :] + grads_land[0].astype(f32)
+    stage_out.start()
+    sums = [finish(piece) for piece in pieces]
     for at in range(5):
         weight_outs[3 + at][...] = sums[0][at * deep : (at + 1) * deep, :]
     for at in range(sums[1].shape[0] // deep):
@@ -1230,9 +1289,6 @@
     for at in range(sums[2].shape[0] // PAIR):
         r = slice(at * PAIR, (at + 1) * PAIR)
         weight_outs[9][r, :] = sums[2][r, :].T
-    arrive([source_cross])
-    stage_s[1] = source_far[...].astype(f32)
-    source_outs[1].start()
     arrive([gain_side])
     gain_planes[plane] = gain_land[3] + gain_far[...]
     begin(gain_last)
@@ -1242,20 +1298,52 @@
         value = value + planes_q[at].astype(f32)
     for at in range(3):
         weight_outs[at][...] = value[at * deep : (at + 1) * deep, :]
-    for row in range(per):
-        arrive([grads_cross[row]])
-        stage[1, row * BLOCK : (row + 1) * BLOCK, :] = cross_land[row].astype(f32)
-    stage_out[1].start()
     arrive(gain_last)
     value = gain_planes[0]
     for at in range(1, planes):
         value = value + gain_planes[at]
     gain_out[...] = value
-    arrive([rows_cross])
-    for copy in [rows_local, *stage_out, *source_outs]:
+    arrive([rows_cross, source_cross, *grads_cross])
+    for copy in (stage_out, source_own):
         copy.wait()
     for copy in semaphores.sent:
         copy.wait_send()
+
+
+def hand_over_kernel(planes, *refs):
+    (rows_any, rows_far, grad_own, grad_far, source_own, source_far, *plain) = refs[:17]
+    (decoder_out, grad_out, source_out, *plain_outs) = refs[17:31]
+    (rows_s, grad_s, grad_low, source_s, source_low, *plain_s) = refs[31:-2]
+    load, store = refs[-2:]
+    chip = Where(planes).chip
+    rows = rows_s.shape[1]
+    moves = [
+        (rows_any.at[:rows], rows_s.at[0], rows_s.at[0], decoder_out.at[chip]),
+        (rows_far, rows_s.at[1], rows_s.at[1], decoder_out.at[1 - chip]),
+        (grad_own, grad_s.at[0], grad_s.at[0], grad_out.at[chip]),
+        (grad_far, grad_low, grad_s.at[1], grad_out.at[1 - chip]),
+        (source_own, source_s.at[0], source_s.at[0], source_out.at[chip]),
+        (source_far, source_low, source_s.at[1], source_out.at[1 - chip]),
+    ]
+    moves += [
+        (one, held, held.at[: other.shape[0]], other)
+        for one, held, other in zip(plain, plain_s, plain_outs)
+    ]
+    loads = [pltpu.make_async_copy(m[0], m[1], load.at[at]) for at, m in enumerate(moves)]
+    stores = [pltpu.make_async_copy(m[2], m[3], store.at[at]) for at, m in enumerate(moves)]
+    for copy in loads:
+        copy.start()
+    for at, (one, other) in enumerate(zip(loads, stores)):
+        one.wait()
+        if at == 3:
+            for row in range(grad_low.shape[0]):
+                size = grad_low.shape[1]
+                grad_s[1, row * size : (row + 1) * size, :] = grad_low[row].astype(f32)
+        if at == 5:
+            source_s[1] = source_low[...].astype(f32)
+        other.start()
+    for copy in stores:
+        copy.wait()
 
 
 def call(kernel, outs, *operands, scratch=(), smem=0, params=PARAMS, spaces=None, out_space=VMEM, out_spaces=None):
@@ -1295,7 +1383,7 @@
 
 
 def gather_plain(arguments, seq_size, dp_size):
-    (decoder_in, source_states, out_grad, narrow, ffn_expand, ffn_reduce, gain_block) = arguments
+    (decoder_in, source_states, out_grad, narrow, ffn_expand, ffn_reduce, norm_gains) = arguments
     chip = lax.axis_index("seq") // 2
     rows_dec = decoder_in.shape[1]
     own = 2 * rows_dec
@@ -1307,7 +1395,7 @@
     other_rows = swapped(own_rows, "seq", 1)
     x_all = jnp.concatenate([own_rows[:own], other_rows[:own]], axis=0)
     source_all = jnp.concatenate([own_rows[own:], other_rows[own:]], axis=0)
-    cotangent = jnp.concatenate([out_grad[chip], swapped(out_grad[1 - chip], "seq", 2)], axis=0)
+    cotangent = swapped(out_grad[1 - chip], "seq", 2)
 
     def whole(weight):
         weight = lax.all_gather(weight, "seq", axis=1, tiled=True)
@@ -1318,6 +1406,7 @@
     later_a = jnp.concatenate(blocks[3:], axis=3)
     later_b = as_blocks(whole(ffn_expand), ffn_expand.shape[1] // PAIR)
     later_c = as_blocks(whole(ffn_reduce))
+    gain_block = jnp.pad(norm_gains.astype(f32), ((0, 5), (0, 0)))
     gains = lax.all_gather(gain_block, "seq", axis=0)
     return x_all, source_all, cotangent, qkv, later_a, later_b, later_c, gains
 
@@ -1355,7 +1444,6 @@
     deep_two = ffn_reduce.shape[0]
     wide = ffn_expand.shape[1] // PAIR
     hidden_width = wide * PAIR * seq_size
-    gain_block = jnp.pad(norm_gains.astype(f32), ((0, 5), (0, 0)))
     all_src = 4 * rows_src
     comm = dp_size == 8
 
@@ -1384,7 +1472,7 @@
         gathered = [
             ((total, width), bf16),
             ((all_src, width), bf16),
-            ((own, width), bf16),
+            ((rows_dec, width), bf16),
             (cut + (3 * deep, PAIR), bf16),
             (cut + (5 * deep, PAIR), bf16),
             (cut + (wide * deep, PAIR), bf16),
@@ -1392,7 +1480,7 @@
             ((seq_size, 8, PAIR), f32),
         ]
         operands = (source_len, upsample, decoder_in, source_states, out_grad)
-        operands += (*narrow, ffn_expand, ffn_reduce, gain_block)
+        operands += (*narrow, ffn_expand, ffn_reduce, norm_gains)
         (
             x_all, source_all, cotangent, qkv, later_a, later_b, later_c, gains,
             q, k, v, mixed, query_extra,
@@ -1406,9 +1494,14 @@
                 VMEM((seq_size, 8, PAIR), f32),
                 *work,
                 *semaphores,
+                VMEM((5 * deep, PAIR), bf16),
+                VMEM((wide * deep, PAIR), bf16),
+                VMEM((deep_two, PAIR), bf16),
+                VMEM((rows_src, width), bf16),
+                VMEM((8, PAIR), f32),
             ],
             smem=2,
-            spaces={at: pl.ANY for at in range(2, len(operands))},
+            spaces={at: pl.ANY for at in range(2, len(operands) - 1)},
             out_space=pl.ANY,
             params=pltpu.CompilerParams(
                 vmem_limit_bytes=VMEM_LIMIT, collective_id=0, has_side_effects=True
@@ -1416,7 +1509,7 @@
         )
     else:
         x_all, source_all, cotangent, qkv, later_a, later_b, later_c, gains = gather_plain(
-            (decoder_in, source_states, out_grad, narrow, ffn_expand, ffn_reduce, gain_block),
+            (decoder_in, source_states, out_grad, narrow, ffn_expand, ffn_reduce, norm_gains),
             seq_size,
             dp_size,
         )
@@ -1453,6 +1546,7 @@
         send_counts,
         x_all,
         mixed,
+        out_grad,
         cotangent,
         source_all,
         later_a,
@@ -1473,7 +1567,8 @@
             VMEM((all_src, PAIR), bf16),
             VMEM(pair_rows(all_src), f32),
             VMEM(pair_rows(all_src), f32),
-            pltpu.SemaphoreType.DMA,
+            pltpu.SemaphoreType.DMA((3,)),
+            VMEM((own, width), bf16),
             VMEM((pairs, BLOCK, PAIR), bf16),
             VMEM((2 * pairs, BLOCK, PAIR), bf16),
             VMEM((pairs, PAIR, BLOCK), bf16),
@@ -1482,7 +1577,7 @@
             VMEM((pairs, BLOCK, PAIR), bf16),
         ],
         smem=3,
-        spaces={3: pl.ANY},
+        spaces={3: pl.ANY, 5: pl.ANY, 6: pl.ANY},
     )
     part_q = ((seq_size, 2, 4, 3 * width // 8, PAIR), bf16)
     operands = (source_len, upsample, q, k, v, mixed, grad_mixed, query_extra)
@@ -1525,7 +1620,7 @@
             *per_piece((2, 2, planes)),
             *per_piece((2, planes)),
             *per_piece((planes,)),
-            *per_piece((planes - 1,)),
+            *per_piece((2, planes - 1)),
             VMEM((3, 2, planes, 3 * deep, PAIR), bf16),
             VMEM((planes, 3 * deep, PAIR), bf16),
             VMEM((planes - 1, 3 * deep, PAIR), bf16),
@@ -1536,24 +1631,22 @@
             VMEM((2, rows_dec, width), bf16),
             VMEM((2, rows_dec, width), bf16),
             VMEM((rows_dec // BLOCK, BLOCK, width), bf16),
-            VMEM((rows_dec // BLOCK, BLOCK, width), bf16),
-            VMEM((2, rows_dec, width), f32),
+            VMEM((rows_dec, width), f32),
             VMEM((2 * rows_src, width), bf16),
             VMEM((2 * rows_src, width), bf16),
-            VMEM((rows_src, width), bf16),
-            VMEM((2, rows_src, width), f32),
+            VMEM((rows_src, width), f32),
         ]
         small = ((deep, PAIR), f32)
+        plain = [small] * 8 + [(ffn_expand.shape, f32), (ffn_reduce.shape, f32), ((8, PAIR), f32)]
         outs = call(
             partial(last_kernel, True, planes),
             [
-                (decoder_in.shape, bf16),
-                (decoder_in.shape, f32),
-                (source_states.shape, f32),
-                *[small] * 8,
-                (ffn_expand.shape, f32),
-                (ffn_reduce.shape, f32),
-                ((8, PAIR), f32),
+                ((rows_dec, width), bf16),
+                ((rows_dec, width), f32),
+                ((rows_dec // BLOCK, BLOCK, width), bf16),
+                ((rows_src, width), f32),
+                ((rows_src, width), bf16),
+                *plain,
             ],
             *operands,
             part_a,
@@ -1564,10 +1657,33 @@
             scratch=work,
             smem=2,
             spaces=everywhere,
-            out_spaces={at: pl.ANY for at in range(3)},
+            out_spaces={at: pl.ANY for at in range(5)},
             params=pltpu.CompilerParams(
                 vmem_limit_bytes=VMEM_LIMIT, collective_id=1, has_side_effects=True
             ),
+        )
+        outs = call(
+            partial(hand_over_kernel, planes),
+            [
+                (decoder_in.shape, bf16),
+                (decoder_in.shape, f32),
+                (source_states.shape, f32),
+                *plain[:-1],
+                (norm_gains.shape, f32),
+            ],
+            out_rows,
+            *outs,
+            scratch=[
+                VMEM(decoder_in.shape, bf16),
+                VMEM(decoder_in.shape, f32),
+                VMEM((rows_dec // BLOCK, BLOCK, width), bf16),
+                VMEM(source_states.shape, f32),
+                VMEM((rows_src, width), bf16),
+                *[VMEM(shape, kind) for shape, kind in plain],
+                *[pltpu.SemaphoreType.DMA((17,))] * 2,
+            ],
+            spaces={at: pl.ANY for at in range(17)},
+            out_space=pl.ANY,
         )
         (decoder_out, grad_decoder, grad_src, dwq, dwk, dwv, *rest, dw1, dw2, dgains) = outs
         dwo, dwcq, dwck, dwcv, dwco = rest

time: 268 us -> 228 us (0.85)
  Pallas kernels: 254 us -> 227 us
  local copies, waits for them, and re-layouts: 12.1 us -> 0 us
    pallas_call x3 -> x4, Pallas kernels: 254 us -> 227 us  [call(): pl.pallas_call(kernel, out_shape=[jax.ShapeDtypeStruct(shape, kind) for s...]
    unnamed x37 -> x0, local copies, waits for them, and re-layouts: 10.7 us -> none
where the time goes in v3:
time: 228 us
  Pallas kernels  227 us (100%)
    pallas_call x4, Pallas kernels, call(): pl.pallas_call(kernel, out_shape=[jax.ShapeDtypeStruct(shape, kind) for s...  227 us

profile of v3, /device:TPU:0, one launch (start us, length us, event | category | flops | bytes accessed | tf_op | source)
XLA Modules:
  0.0 227.7 jit_solution(13865753238415321659)
XLA Ops:
  0.7 64.3 %shard_map.272 = (bf16[2048,512]{1,0:T(8,128)(2,1)}, bf16[512,512]{1,0:T(8,128)(2,1)}, bf16[512,512]{1,0:T(8,128)(2,1)}, bf16[4,2,4,192,128]{4,3,2,1,0:T(8,128)(...) custom-call(s32[16]{0:T(128)} %source_len_ref.5, ...), custom_call_target="tpu_custom_call" | custom-call | tf_op jit(solution)/shard_map/pallas_call | solution.py:1352
  65.0 68.6 %shard_map.273 = (bf16[1024,512]{1,0:T(8,128)(2,1)}, bf16[4,1024,128]{2,1,0:T(8,128)(2,1)}, f32[1024,512]{1,0:T(8,128)}, bf16[4,2,4,320,128]{4,3,2,1,0:T(8,128)(...) custom-call(s32[16]{0:T(128)} %source_len_ref.5, ...), custom_call_target="tpu_custom_call" | custom-call | tf_op jit(solution)/shard_map/pallas_call | solution.py:1352
  133.6 90.4 %shard_map.274 = (bf16[512,512]{1,0:T(8,128)(2,1)}, f32[512,512]{1,0:T(8,128)}, bf16[2,256,512]{2,1,0:T(8,128)(2,1)}, f32[128,512]{1,0:T(8,128)}, bf16[128,512]{...) custom-call(s32[16]{0:T(128)} %source_len_ref.5, ...), custom_call_target="tpu_custom_call" | custom-call | tf_op jit(solution)/shard_map/pallas_call | solution.py:1352
  224.0 3.5 %shard_map.275 = (bf16[2,512,512]{2,1,0:T(8,128)(2,1)}, f32[2,512,512]{2,1,0:T(8,128)}, f32[2,128,512]{2,1,0:T(8,128)}, f32[64,128]{1,0:T(8,128)}, f32[64,128]{1...) custom-call(bf16[1024,512]{1,0:T(8,128)(2,1)} %get-tuple-element.59., ...), custom_call_target="tpu_custom_call" | custom-call | tf_op jit(solution)/shard_map/pallas_call | solution.py:1352
